TPU v7x, 256 devices: a whole 4x4x8 slice. The times are simulated.
256 devices in a mesh: gx: 8 (over x, y_hi), gy: 32 (over y_lo, z, core).
Axes of the slice: x: 4, y: 4 (y_hi: 2, y_lo: 2; y = y_hi * 2 + y_lo), z: 8, core: 2. Of those that a mesh axis runs over, the one named last changes fastest.
Arguments:
- tensor: bfloat16 [2, 512, 1024, 1024], P(None, 'gy', 'gx'), may hold values from -6 to 6
- row_factor: float32 [96, 1024], P(None, ('gx', 'gy')), may hold values from -4 to 4
- column_factor: float32 [96, 1024], P(None, 'gy'), may hold values from -4 to 4
- band_factor: float32 [96, 512], P(None, ('gy', 'gx')), may hold values from -4 to 4
- time_factor: float32 [96, 2], replicated, may hold values from -4 to 4
Outputs:
- row_grad: float32 [96, 1024], P(None, ('gx', 'gy'))
- column_grad: float32 [96, 1024], P(None, 'gy')
- band_grad: float32 [96, 512], P(None, ('gy', 'gx'))
- time_grad: float32 [96, 2], replicated
All inputs are finite; a program needn't handle non-finite values.
Results may differ from a plain program's by a relative error of at most 0.0028.
Values sent between devices are 32-bit elements; how exact they have to be, the bound alone decides.
A program may use at most 64 MiB of HBM per device.

v0:
```python
import jax
import jax.numpy as jnp
from jax import lax
from jax.sharding import PartitionSpec as P


def gram_of(factor):
    return jnp.dot(
        factor, factor.T, precision=lax.Precision.HIGHEST, preferred_element_type=jnp.float32
    )


def shards(tensor, row_factor, column_factor, band_factor, time_factor):
    highest = lax.Precision.HIGHEST
    frames, bands_here, rows_here, columns = tensor.shape
    rank_rows = row_factor.shape[0]
    row_block = lax.all_gather(row_factor, "gy", axis=1, tiled=True)
    band_block = lax.all_gather(band_factor, "gx", axis=1, tiled=True)
    col_whole = lax.all_gather(column_factor, "gy", axis=1, tiled=True)
    flattened = tensor.reshape(frames * bands_here * rows_here, columns)
    low_cols = col_whole.astype(jnp.bfloat16)
    folded = lax.dot_general(
        low_cols, flattened, (((1,), (1,)), ((), ())), preferred_element_type=jnp.float32
    )
    folded = folded.reshape(rank_rows, frames, bands_here, rows_here)
    by_time = jnp.einsum("rtbi,rt->rbi", folded, time_factor, precision=highest)
    by_band = jnp.einsum("rtbi,rb->rti", folded, band_block, precision=highest)
    rows_part = jnp.einsum("rbi,rb->ri", by_time, band_block, precision=highest)
    bands_part = jnp.einsum("rbi,ri->rb", by_time, row_block, precision=highest)
    frames_part = jnp.einsum("rti,ri->rt", by_band, row_block, precision=highest)
    product = (
        time_factor[:, :, None, None] * band_block[:, None, :, None] * row_block[:, None, None, :]
    ).astype(jnp.bfloat16)
    product = product.reshape(rank_rows, frames * bands_here * rows_here)
    cols_part = jnp.dot(product, flattened, preferred_element_type=jnp.float32)
    row_width = row_factor.shape[1]
    band_width = band_factor.shape[1]
    col_width = column_factor.shape[1]
    rows_sum = lax.psum(rows_part, "gy")
    rows_mine = lax.dynamic_slice_in_dim(rows_sum, lax.axis_index("gy") * row_width, row_width, 1)
    bands_sum = lax.psum(bands_part, "gx")
    bands_mine = lax.dynamic_slice_in_dim(
        bands_sum, lax.axis_index("gx") * band_width, band_width, 1
    )
    cols_sum = lax.psum(cols_part, ("gx", "gy"))
    cols_mine = lax.dynamic_slice_in_dim(cols_sum, lax.axis_index("gy") * col_width, col_width, 1)
    gram_cols = gram_of(col_whole)
    gram_rows = lax.psum(gram_of(row_block), "gx")
    gram_bands = lax.psum(gram_of(band_block), "gy")
    frames_term = lax.psum(frames_part, ("gx", "gy"))
    gram_time = gram_of(time_factor)
    row_grad = (
        jnp.dot(gram_cols * gram_bands * gram_time, row_factor, precision=highest) - rows_mine
    )
    column_grad = (
        jnp.dot(gram_rows * gram_bands * gram_time, column_factor, precision=highest) - cols_mine
    )
    band_grad = (
        jnp.dot(gram_rows * gram_cols * gram_time, band_factor, precision=highest) - bands_mine
    )
    time_grad = (
        jnp.dot(gram_rows * gram_cols * gram_bands, time_factor, precision=highest) - frames_term
    )
    return (row_grad, column_grad, band_grad, time_grad)


def solution(mesh):
    return jax.shard_map(
        shards,
        mesh=mesh,
        in_specs=(
            P(None, "gy", "gx", None),
            P(None, ("gx", "gy")),
            P(None, "gy"),
            P(None, ("gy", "gx")),
            P(),
        ),
        out_specs=(P(None, ("gx", "gy")), P(None, "gy"), P(None, ("gy", "gx")), P()),
        check_vma=False,
    )
```

profile of v0, /device:TPU:1, one launch (start us, length us, event | category | flops | bytes accessed | tf_op | source)
XLA Modules:
  0.0 537.8 jit_solution(16476500216602893297)
XLA Ops:
  7.2 0.0 all-reduce.7.cloned.1.call-start
  7.2 40.2 %all_gather.9 = f32[96,1024]{0,1:T(8,128)S(1)} all-gather(f32[96,32]{0,1:T(8,128)} %param.7), channel_id=1, replica_groups=mesh['gx'=8,'gy'=32] {'gy'}, dimensions={1}, use_global_device_ids=true | all-gather | bytes 405504 | tf_op jit(solution)/shard_map/all_gather | solution.py:19
  47.4 19.7 %all-gather = f32[8,2,96]{2,1,0:T(2,128)S(1)} all-gather(f32[1,2,96]{2,1,0:T(2,128)} %bitcast.59), channel_id=1, replica_groups=mesh['gx'=8,'gy'=32] {'gx'}, dimensions={0}, use_global_device_ids=true | all-gather | bytes 6912 | tf_op jit(solution)/shard_map/all_gather | solution.py:18
  67.1 0.9 fusion.18
  68.0 0.8 copy.17
  68.8 0.1 copy.12
  68.9 0.1 copy.38
  69.0 6.1 %fusion.6 = f32[96,2,16,128]{3,0,2,1:T(8,128)S(1)} fusion(bf16[2,16,128,1024]{3,2,1,0:T(8,128)(2,1)} %param.5, bf16[96,1024]{1,0:T(8,128)(2,1)S(1)} %copy.12), kind=kOutput, calls=%fused_computation.14 | convolution fusion | flops 805306368 | bytes 10158080 | tf_op jit(solution)/shard_map/dot_general | solution.py:22
  75.0 0.0 copy-start.1
  75.1 0.0 copy-start.2
  75.1 6.0 %fusion.2 = f32[96,1,16,128]{3,1,2,0:T(1,128)S(1)} fusion(f32[96,2,1,1]{1,2,3,0:T(1,128)S(1)} %copy.17, f32[96,2,16,128]{3,0,2,1:T(8,128)S(1)} %fusion.6), kind=kOutput, calls=%fused_computation.3 | convolution fusion | flops 4718592 | bytes 2360064 | tf_op jit(solution)/shard_map/rtbi,rt->rbi/dot_general | solution.py:26
  81.1 0.3 multiply_reduce_fusion.1
  81.4 0.7 copy.22
  82.1 0.0 all-reduce.7.cloned.1.call-update
  82.2 0.0 all-reduce.5.cloned.1.call-start
  82.2 0.0 copy-done.1
  82.2 0.0 copy-done.2
  82.2 34.5 %all-gather.1 = f32[32,4,96]{2,1,0:T(4,128)S(1)} all-gather(f32[1,4,96]{2,1,0:T(4,128)S(1)} %bitcast.58), channel_id=1, replica_groups=mesh['gx'=8,'gy'=32] {'gy'}, dimensions={0}, use_global_device_ids=true | all-gather | bytes 50688 | tf_op jit(solution)/shard_map/all_gather | solution.py:17
  116.7 0.1 copy.13
  116.8 8.0 %convolution_bitcast_fusion = f32[96,1024]{0,1:T(8,128)} fusion(bf16[2,16,128,1024]{3,2,1,0:T(8,128)(2,1)} %param.5, f32[96,128]{1,0:T(8,128)S(1)} %copy.13, f32[96,2,16]{0,2,1:T(8,128)S(1)} %broadcast_multiply_fusion), kind=kOutput, calls=%fused_computation.5 | convolution fusion | flops 806092800 | bytes 8843264 | tf_op jit(solution)/shard_map/dot_general | solution.py:35
  124.8 0.0 all-reduce.5.cloned.1.call-update
  124.8 0.3 fusion.19
  125.1 1.0 fusion.17
  126.1 0.3 fusion.20
  126.4 0.0 copy-start.3
  126.4 0.0 copy-start
  126.4 0.3 multiply_reduce_fusion
  126.7 0.1 copy.29
  126.7 0.1 copy.31
  126.8 1.9 fusion
  128.7 0.2 multiply_reduce_fusion.2
  128.9 0.1 copy.37
  129.0 73.5 %psum.47 = f32[96,2]{0,1:T(2,128)S(1)} all-reduce(f32[96,2]{0,1:T(2,128)S(1)} %copy.37), channel_id=1, replica_groups=mesh['gx'=8,'gy'=32] {'gx','gy'}, use_global_device_ids=true, to_apply=%region_5.0 | all-reduce | flops 192 | bytes 1536 | tf_op jit(solution)/shard_map/psum | solution.py:50
  202.5 31.1 %all-reduce.1 = (f32[96,96]{1,0:T(8,128)S(1)}, f32[96,16]{0,1:T(8,128)S(1)}) all-reduce(f32[96,96]{1,0:T(8,128)S(1)} %fusion.20, f32[96,16]{0,1:T(8,128)S(1)} %copy.29), channel_id=1, replica_groups=mesh['gx'=8,'gy'=32] {'gx'}, use_global_device_ids=true, to_apply=%region_2.0 | all-reduce | flops 10752 | bytes 86016 | tf_op jit(solution)/shard_map/psum | solution.py:48
  233.6 0.0 copy-done.3
  233.7 0.8 convolution_subtract_fusion.3
  234.4 38.6 %all-reduce.7.cloned.1.call-done = (f32[96,96]{1,0:T(8,128)}, f32[96,128]{0,1:T(8,128)}) async-done(((f32[96,96]{1,0:T(8,128)}, f32[96,128]{0,1:T(8,128)}), (f32[96,96]{1,0:T(8,128)}, f32[96,128]{0,1:T(8,128)})) %all-reduce.7.cloned.1.call-update) | async-done | bytes 86032 | tf_op jit(solution)/shard_map/psum | solution.py:49
  273.0 1.6 convolution_subtract_fusion.1
  274.6 1.6 convolution_subtract_fusion.2
  276.2 253.1 %all-reduce.5.cloned.1.call-done = f32[96,1024]{0,1:T(8,128)} async-done(((f32[96,1024]{0,1:T(8,128)}), f32[96,1024]{0,1:T(8,128)}) %all-reduce.5.cloned.1.call-update) | async-done | bytes 393232 | tf_op jit(solution)/shard_map/psum | solution.py:45
  529.3 0.0 copy-done
  529.3 1.6 convolution_subtract_fusion
  (1 shorter events, 0.0 us)
Async XLA Ops:
  7.2 265.9 %all-reduce.7.cloned.1.call-start = ((), (), s32[]{:S(2)}) async-start(), calls=%async_computation.1 | async-start | bytes 229376 | tf_op jit(solution)/shard_map/psum | solution.py:49
  75.0 7.2 %copy-start.1 = (f32[96,2]{0,1:T(2,128)S(1)}, f32[96,2]{0,1:T(2,128)}, u32[]{:S(2)}) copy-start(f32[96,2]{0,1:T(2,128)} %param.9) | copy-start | bytes 2308
  75.1 7.2 %copy-start.2 = (f32[96,4]{0,1:T(4,128)S(1)}, f32[96,4]{0,1:T(4,128)}, u32[]{:S(2)}) copy-start(f32[96,4]{0,1:T(4,128)} %param.6) | copy-start | bytes 4612
  82.2 447.2 %all-reduce.5.cloned.1.call-start = ((), (), s32[]{:S(2)}) async-start(), calls=%async_computation | async-start | bytes 1048576 | tf_op jit(solution)/shard_map/psum | solution.py:45
  126.4 107.3 %copy-start.3 = (f32[96,2]{0,1:T(2,128)S(1)}, f32[96,2]{0,1:T(2,128)}, u32[]{:S(2)}) copy-start(f32[96,2]{0,1:T(2,128)} %param.8) | copy-start | bytes 2308
  126.4 402.9 %copy-start = (f32[96,32]{0,1:T(8,128)S(1)}, f32[96,32]{0,1:T(8,128)}, u32[]{:S(2)}) copy-start(f32[96,32]{0,1:T(8,128)} %param.7) | copy-start | bytes 36868
Sparse Core Ops, SparseCore 0:
  82.3 190.7 all-reduce.6
  279.4 249.8 all-reduce.4
where the time goes:
time: 539 us; the launch traced here: 538 us
  waiting for transfers between devices  292 us (54%)
  blocking collectives  199 us (37%)
  matrix products  29.9 us (6%)
  between operations  14.2 us (3%)
    psum x1, waiting for transfers between devices, shards(): cols_sum = lax.psum(cols_part, ('gx', 'gy'))  253 us
    psum x1, blocking collectives, shards(): frames_term = lax.psum(frames_part, ('gx', 'gy'))  73.5 us
    all_gather x1, blocking collectives, shards(): col_whole = lax.all_gather(column_factor, 'gy', axis=1, tiled=True)  40.2 us
    psum x1, waiting for transfers between devices, shards(): gram_bands = lax.psum(gram_of(band_block), 'gy')  38.6 us
    all_gather x1, blocking collectives, shards(): row_block = lax.all_gather(row_factor, 'gy', axis=1, tiled=True)  34.5 us
    psum x1, blocking collectives, shards(): gram_rows = lax.psum(gram_of(row_block), 'gx')  31.1 us
    all_gather x1, blocking collectives, shards(): band_block = lax.all_gather(band_factor, 'gx', axis=1, tiled=True)  19.7 us
  transfers between devices with their start and end apart: 2, of which 2 were waited for; matrix products, arithmetic and copies ran while one was open for 3% of the time, Pallas kernels for 0%

commit v1 on v0

v1 whole, which is shorter than its diff:
```python
import jax
import jax.numpy as jnp
from jax import lax
from jax.experimental import pallas as pl
from jax.experimental.pallas import tpu as pltpu
from jax.sharding import PartitionSpec as P

MESH = pl.DeviceIdType.MESH
HIGHEST = lax.Precision.HIGHEST
F32 = jnp.float32
BF16 = jnp.bfloat16

NX, NY, NLZ = 8, 32, 16
RANK, LANES = 96, 128
FRAMES, BANDS, ROWS, COLS = 2, 16, 128, 1024
RW, CW, BW = 4, 32, 2
PACK = CW * RANK // LANES
TB = FRAMES * BANDS
HALF = BANDS * ROWS
CHUNKS = 2
CHUNK = COLS // CHUNKS
PER = NLZ // CHUNKS
LOADS = 8
MSG = CW + 8
QROWS = ROWS // 4

(
    S_ROW, S_BAND, S_BANDX, S_COL, S_COLC, S_R1, S_R2, S_R3, S_F1, S_F2,
    S_GRAM, S_GRAMP, S_ROWS, S_BANDS,
) = [0, 1, 2, 3, 4, 5, 7, 8, 9, 10, 11, 12, 13, 14]
N_SEMS = 15


def dot(x, y):
    return jnp.dot(x, y, preferred_element_type=F32)


def exact(x, y):
    return jnp.dot(x, y, precision=HIGHEST, preferred_element_type=F32)


def total(ref, count):
    out = ref[0]
    for k in range(1, count):
        out = out + ref[k]
    return out


def wrap(index, size):
    return jnp.where(index >= size, index - size, index)


def lane_of(x):
    return lax.broadcasted_iota(jnp.int32, x.shape, 1)


def pack(tiles):
    spare = lane_of(tiles[3]) >= RANK
    return [
        jnp.where(spare, pltpu.roll(tiles[3], RANK - 32 * m, 1), tiles[m]) for m in range(3)
    ]


def unpack(tiles):
    lane = lane_of(tiles[0])
    last = jnp.zeros_like(tiles[0])
    for m in (2, 1, 0):
        last = jnp.where(lane < 32 * m + 32, pltpu.roll(tiles[m], 32 * m + 32, 1), last)
    zero = jnp.zeros_like(last)
    return [jnp.where(lane < RANK, tile, zero) for tile in tiles] + [
        jnp.where(lane < RANK, last, zero)
    ]


def kernel(
    tensor, packed,
    out,
    data, mine4, mine2, rowg, bandg, bandx, row_t, band_t, bandx_t, tb_t,
    turned, prod, by_frame, part, recv1, sum1, recv2, fin, recv3,
    colg, colf, low, folded, partials,
    fpart, fg, fsum, fx, gpart, grecv, gall, gcols,
    rsend, rrecv, bsend, brecv,
    local_sems, send_sems, recv_sems,
):
    a = lax.axis_index("gx")
    g = lax.axis_index("gy")
    lz = lax.div(g, 2)
    c = g - 2 * lz
    l = lax.div(lz, 8)
    z = lz - 8 * l
    p = l * 2 + c
    other = 1 - c
    partner = lz * 2 + other
    gy_peers = [wrap(g + k, NY) for k in range(1, NY)]
    gx_peers = [wrap(a + k, NX) for k in range(1, NX)]
    core_peers = [wrap(lz + k, NLZ) * 2 + c for k in range(1, NLZ)]

    def send(src, dst, sem, device):
        pltpu.make_async_remote_copy(
            src_ref=src, dst_ref=dst, send_sem=send_sems.at[sem], recv_sem=recv_sems.at[sem],
            device_id=device, device_id_type=MESH,
        ).start()

    def arrived(ref, sem):
        pltpu.make_async_copy(ref, ref, recv_sems.at[sem]).wait()

    def sent(ref, sem):
        pltpu.make_async_copy(ref, ref, send_sems.at[sem]).wait()

    barrier = pltpu.get_barrier_semaphore()
    for to in gy_peers:
        pl.semaphore_signal(barrier, inc=1, device_id=(a, to), device_id_type=MESH)
    for to in gx_peers:
        pl.semaphore_signal(barrier, inc=1, device_id=(to, g), device_id_type=MESH)

    for k in range(LOADS):
        span = pl.ds(k * (TB // LOADS), TB // LOADS)
        pltpu.make_async_copy(tensor.at[span], data.at[span], local_sems.at[k]).start()

    tb_t[...] = jnp.zeros_like(tb_t)
    mine2[...] = packed[CW : CW + BW]
    mine4[...] = packed[MSG : MSG + RW]
    time8 = packed[MSG + 8 :]
    rowg[g] = mine4[...]
    bandg[a] = mine2[...]
    bandx[g] = mine2[...]
    for m, tile in enumerate(pack([packed[8 * m : 8 * m + 8] for m in range(4)])):
        colg[c, lz, 8 * m : 8 * m + 8] = tile

    pl.semaphore_wait(barrier, NY - 1 + NX - 1)

    for to in gy_peers:
        send(mine4, rowg.at[g], S_ROW, (a, to))
    for to in gx_peers:
        send(mine2, bandg.at[a], S_BAND, (to, g))
    for to in core_peers:
        send(colg.at[c, lz], colg.at[c, lz], S_COL, (a, to))
    for to in gy_peers:
        send(mine2, bandx.at[g], S_BANDX, (a, to))

    @pl.loop(0, LOADS)
    def _(k):
        per = TB // LOADS
        span = pl.ds(k * per, per)
        pltpu.make_async_copy(tensor.at[span], data.at[span], local_sems.at[k]).wait()
        for i in range(per):
            at = pl.multiple_of((k * per + i) * ROWS, ROWS)
            turned[:, pl.ds(at, ROWS)] = data[k * per + i].T

    arrived(bandg.at[pl.ds(0, NX - 1)], S_BAND)
    for k in range(NX):
        band_t[BW * k : BW * k + BW] = bandg[k]
    for t in range(FRAMES):
        tb_t[t * BANDS : (t + 1) * BANDS] = time8[t : t + 1] * band_t[...]
    tb_t[TB : TB + BANDS] = band_t[...]
    arrived(rowg.at[pl.ds(0, NY - 1)], S_ROW)
    for k in range(NY):
        row_t[RW * k : RW * k + RW] = rowg[k]

    @pl.loop(0, BANDS)
    def _(k):
        span = pl.ds(pl.multiple_of(k * ROWS, ROWS), ROWS)
        rows = row_t[...]
        plain = (tb_t[pl.ds(TB + k, 1)] * rows).astype(BF16)
        for t in range(FRAMES):
            prod[t, span, 0:LANES] = (tb_t[pl.ds(t * BANDS + k, 1)] * rows).astype(BF16)
            prod[t, span, LANES:] = plain

    def send_pieces(n):
        span = pl.ds(n * PER, PER)
        arrived(recv1.at[span], S_R1 + n)
        sum1[span] = part[c, span] + recv1[span]
        for i in range(PER):
            k = n * PER + i

            @pl.when(k != lz)
            def _():
                send(sum1.at[k], recv2.at[lz], S_R2, (a, k * 2 + c))

    @pl.loop(0, CHUNKS)
    def _(n):
        here = pl.ds(pl.multiple_of(n * CHUNK, CHUNK), CHUNK)
        acc = jnp.zeros((CHUNK, LANES), F32)
        for t in range(FRAMES):
            both = dot(turned[here, t * HALF : (t + 1) * HALF], prod[t])
            by_frame[t, here] = both[:, LANES:]
            acc = acc + both[:, 0:LANES]
        acc = acc.reshape(CHUNK // CW, 4, 8, LANES)
        tiles = pack([acc[:, m].reshape(CHUNK // 4, LANES) for m in range(4)])
        for k in range(CHUNK // CW):
            for m in range(3):
                part[k % 2, n * PER + k // 2, 8 * m : 8 * m + 8] = tiles[m][8 * k : 8 * k + 8]
        span = pl.ds(n * PER, PER)
        send(part.at[other, span], recv1.at[span], S_R1 + n, (a, partner))

        @pl.when(n > 0)
        def _():
            send_pieces(n - 1)

    arrived(colg.at[0, pl.ds(0, NLZ - 1)], S_COL)
    send(colg.at[c], colg.at[c], S_COLC, (a, partner))

    arrived(bandx.at[pl.ds(0, NY - 1)], S_BANDX)
    for k in range(NY):
        bandx_t[BW * k : BW * k + BW] = bandx[k]
    for i, ref in enumerate((row_t, bandx_t)):
        gram = exact(ref[...].T, ref[...])
        for k in range(4):
            gpart[k, i] = gram[24 * k : 24 * k + 24]
    grecv[a] = gpart[p]
    send_pieces(CHUNKS - 1)
    for to in gx_peers:
        send(gpart.at[p], grecv.at[a], S_GRAM, (to, g))

    arrived(colg.at[0], S_COLC)
    for i in range(2):
        tiles = unpack(
            [colg[i, :, 8 * m : 8 * m + 8].reshape(8 * NLZ, LANES) for m in range(3)]
        )
        for k in range(NLZ):
            block = jnp.concatenate([tile[8 * k : 8 * k + 8] for tile in tiles], axis=0)
            at = (2 * k + i) * CW
            colf[at : at + CW] = block
            low[at : at + CW] = block.astype(BF16)

    for t in range(FRAMES):
        fpart[t : t + 1] = jnp.sum(
            by_frame[t] * low[...].astype(F32), axis=0, keepdims=True
        )
    fg[g] = fpart[...]
    for to in gy_peers:
        send(fpart, fg.at[g], S_F1, (a, to))

    @pl.loop(0, 4)
    def _(q):
        here = pl.ds(pl.multiple_of(q * QROWS, QROWS), QROWS)
        folded[...] = dot(data[:, here, :].reshape(TB * QROWS, COLS), low[...])
        rows = jnp.zeros((QROWS, LANES), F32)
        row_here = row_t[here]
        for j in range(TB):
            block = folded[j * QROWS : (j + 1) * QROWS]
            rows = rows + block * tb_t[j : j + 1]
            block = block * row_here
            partials[q, j] = jnp.sum(block.reshape(QROWS // 8, 8, LANES), axis=0)
        for i in range(NY // 4):
            rsend[q * (NY // 4) + i] = rows[RW * i : RW * i + RW]
        for i in range(NY // 4):
            k = q * (NY // 4) + i

            @pl.when(k != g)
            def _():
                send(rsend.at[k], rrecv.at[g], S_ROWS, (a, k))

    sums = total(partials, 4)
    bands = jnp.zeros((BANDS, LANES), F32)
    for t in range(FRAMES):
        bands = bands + time8[t : t + 1] * jnp.sum(sums[t * BANDS : (t + 1) * BANDS], axis=1)
    for k in range(NX):
        bsend[k] = bands[BW * k : BW * k + BW]
    for k in range(1, NX):
        to = wrap(a + k, NX)
        send(bsend.at[to], brecv.at[a], S_BANDS, (to, g))
    brecv[a] = bsend[a]
    rrecv[g] = rsend[g]

    arrived(grecv.at[pl.ds(0, NX - 1)], S_GRAM)
    gall[p] = total(grecv, NX)
    for k in range(1, 4):
        to = wrap(p + k, 4)
        to_l = lax.div(to, 2)
        send(gall.at[p], gall.at[p], S_GRAMP, (a, (to_l * 8 + z) * 2 + to - 2 * to_l))
    arrived(fg.at[pl.ds(0, NY - 1)], S_F1)
    fsum[...] = total(fg, NY)
    fx[a] = fsum[...]
    for to in gx_peers:
        send(fsum, fx.at[a], S_F2, (to, g))
    recv2[lz] = sum1[lz]
    arrived(recv2.at[pl.ds(0, NLZ - 1)], S_R2)
    fin[...] = total(recv2, NLZ)
    recv3[a] = fin[...]
    for to in gx_peers:
        send(fin, recv3.at[a], S_R3, (to, g))

    gcols[...] = jnp.zeros_like(gcols)

    @pl.loop(0, 4)
    def _(i):
        block = colf[pl.ds(pl.multiple_of(i * 256, 256), 256)]
        gcols[...] += exact(block.T, block)

    gram_cols = gcols[...]
    arrived(gall.at[pl.ds(0, 3)], S_GRAMP)
    pad = jnp.zeros((LANES - RANK, LANES), F32)
    gram_rows, gram_bands = (
        jnp.concatenate([gall[:, i].reshape(RANK, LANES), pad], axis=0) for i in range(2)
    )
    time_n = jnp.concatenate([time8, jnp.zeros((LANES - 8, LANES), F32)], axis=0).T
    gram_time = time_n[:, 0:1] * time8[0:1] + time_n[:, 1:2] * time8[1:2]
    row_model = exact(packed[MSG : MSG + 8], gram_cols * gram_bands * gram_time)
    col_model = exact(packed[0:CW], gram_rows * gram_bands * gram_time)
    band_model = exact(packed[CW:MSG], gram_rows * gram_cols * gram_time)
    time_model = exact(time8, gram_rows * gram_cols * gram_bands)

    arrived(fx.at[pl.ds(0, NX - 1)], S_F2)
    out[CW : CW + FRAMES] = time_model[0:FRAMES] - total(fx, NX)
    arrived(recv3.at[pl.ds(0, NX - 1)], S_R3)
    sums = total(recv3, NX)
    sums = jnp.concatenate(unpack([sums[8 * m : 8 * m + 8] for m in range(3)]), axis=0)
    out[0:CW] = col_model - sums
    arrived(rrecv.at[pl.ds(0, NY - 1)], S_ROWS)
    out[CW + 8 : CW + 8 + RW] = row_model[0:RW] - total(rrecv, NY)
    arrived(brecv.at[pl.ds(0, NX - 1)], S_BANDS)
    out[CW + 16 : CW + 16 + BW] = band_model[0:BW] - total(brecv, NX)

    sent(rowg.at[pl.ds(0, NY - 1)], S_ROW)
    sent(bandg.at[pl.ds(0, NX - 1)], S_BAND)
    sent(bandx.at[pl.ds(0, NY - 1)], S_BANDX)
    sent(colg.at[0, pl.ds(0, NLZ - 1)], S_COL)
    sent(colg.at[0], S_COLC)
    for n in range(CHUNKS):
        sent(recv1.at[pl.ds(n * PER, PER)], S_R1 + n)
    sent(recv2.at[pl.ds(0, NLZ - 1)], S_R2)
    sent(recv3.at[pl.ds(0, NX - 1)], S_R3)
    sent(fg.at[pl.ds(0, NY - 1)], S_F1)
    sent(fx.at[pl.ds(0, NX - 1)], S_F2)
    sent(grecv.at[pl.ds(0, NX - 1)], S_GRAM)
    sent(gall.at[pl.ds(0, 3)], S_GRAMP)
    sent(rrecv.at[pl.ds(0, NY - 1)], S_ROWS)
    sent(brecv.at[pl.ds(0, NX - 1)], S_BANDS)


def shards(tensor, row_factor, column_factor, band_factor, time_factor):
    v = pltpu.VMEM
    packed = jnp.zeros((MSG + 16, LANES), F32)
    pieces = ((0, column_factor), (CW, band_factor), (MSG, row_factor), (MSG + 8, time_factor))
    for at, x in pieces:
        x = x.T
        packed = packed + jnp.pad(x, ((at, MSG + 16 - at - x.shape[0]), (0, LANES - RANK)))
    out = pl.pallas_call(
        kernel,
        out_shape=jax.ShapeDtypeStruct((CW + 24, LANES), F32),
        in_specs=[pl.BlockSpec(memory_space=pl.ANY), pl.BlockSpec(memory_space=v)],
        out_specs=pl.BlockSpec(memory_space=v),
        scratch_shapes=[
            v((TB, ROWS, COLS), BF16),
            v((RW, LANES), F32),
            v((BW, LANES), F32),
            v((NY, RW, LANES), F32),
            v((NX, BW, LANES), F32),
            v((NY, BW, LANES), F32),
            v((ROWS, LANES), F32),
            v((BANDS, LANES), F32),
            v((NY * BW, LANES), F32),
            v((LANES, LANES), F32),
            v((COLS, TB * ROWS), BF16),
            v((FRAMES, HALF, 2 * LANES), BF16),
            v((FRAMES, COLS, LANES), F32),
            v((2, NLZ, PACK, LANES), F32),
            v((NLZ, PACK, LANES), F32),
            v((NLZ, PACK, LANES), F32),
            v((NLZ, PACK, LANES), F32),
            v((PACK, LANES), F32),
            v((NX, PACK, LANES), F32),
            v((2, NLZ, PACK, LANES), F32),
            v((COLS, LANES), F32),
            v((COLS, LANES), BF16),
            v((TB * QROWS, LANES), F32),
            v((4, TB, 8, LANES), F32),
            v((FRAMES, LANES), F32),
            v((NY, FRAMES, LANES), F32),
            v((FRAMES, LANES), F32),
            v((NX, FRAMES, LANES), F32),
            v((4, 2, 24, LANES), F32),
            v((NX, 2, 24, LANES), F32),
            v((4, 2, 24, LANES), F32),
            v((LANES, LANES), F32),
            v((NY, RW, LANES), F32),
            v((NY, RW, LANES), F32),
            v((NX, BW, LANES), F32),
            v((NX, BW, LANES), F32),
            pltpu.SemaphoreType.DMA((LOADS,)),
            pltpu.SemaphoreType.DMA((N_SEMS,)),
            pltpu.SemaphoreType.DMA((N_SEMS,)),
        ],
        compiler_params=pltpu.CompilerParams(
            collective_id=0, has_side_effects=True, vmem_limit_bytes=48 * 1024 * 1024
        ),
        cost_estimate=pl.CostEstimate(
            flops=4 * RANK * TB * ROWS * COLS, bytes_accessed=2 * TB * ROWS * COLS, transcendentals=0
        ),
    )(
        tensor.reshape(TB, ROWS, COLS),
        packed,
    )
    places = ((CW + 8, RW), (0, CW), (CW + 16, BW), (CW, FRAMES))
    return tuple(out[at : at + n, 0:RANK].T for at, n in places)


def solution(mesh):
    return jax.shard_map(
        shards,
        mesh=mesh,
        in_specs=(
            P(None, "gy", "gx", None),
            P(None, ("gx", "gy")),
            P(None, "gy"),
            P(None, ("gy", "gx")),
            P(),
        ),
        out_specs=(P(None, ("gx", "gy")), P(None, "gy"), P(None, ("gy", "gx")), P()),
        check_vma=False,
    )
```

time: 539 us -> 37.9 us (0.07)
  waiting for transfers between devices: 292 us -> 0 us
  blocking collectives: 199 us -> 0 us
  Pallas kernels: 0 us -> 34.5 us
  matrix products: 29.9 us -> 0 us
  between operations: 14.2 us -> 0.64 us
    psum x2 -> x0, waiting for transfers between devices: 292 us -> none  [the longest x1 253 us: shards(): cols_sum = lax.psum(cols_part, ('gx', 'gy'))]
    psum x2 -> x0, blocking collectives: 105 us -> none  [the longest x1 73.5 us: shards(): frames_term = lax.psum(frames_part, ('gx', 'gy'))]
    all_gather x3 -> x0, blocking collectives: 94.4 us -> none  [the longest x1 40.2 us: shards(): col_whole = lax.all_gather(column_factor, 'gy', axis=1, tiled=True)]
    pallas_call x0 -> x1, Pallas kernels: none -> 34.5 us  [shards(): pl.pallas_call(kernel, out_shape=jax.ShapeDtypeStruct((CW + 24, LANES), F...]
    dot_general x12 -> x0, matrix products: 29.9 us -> none  [the longest x1 7.97 us: shards(): cols_part = jnp.dot(product, flattened, preferred_element_type=jnp.float32)]
  transfers between devices with their start and end apart: 2 -> 0, of which waited for: 2 -> 0; matrix products, arithmetic and copies ran while one was open for 3% -> 0% of each run, Pallas kernels for 0% -> 0%
where the time goes in v1:
time: 37.9 us; the launch traced here: 37.7 us
  Pallas kernels  34.5 us (91%)
  local copies, waits for them, and re-layouts  1.75 us (5%)
  other arithmetic  0.77 us (2%)
  between operations  0.64 us (2%)
    pallas_call x1, Pallas kernels, shards(): pl.pallas_call(kernel, out_shape=jax.ShapeDtypeStruct((CW + 24, LANES), F...  34.5 us
    transpose x3, local copies, waits for them, and re-layouts, shards(): return tuple((out[at:at + n, 0:RANK].T for at, n in places))  1.75 us
    add x1, other arithmetic, shards(): packed + jnp.pad(x, ((at, MSG + 16 - at - x.shape[0]), (0, LANES - RANK)))  0.77 us

profile of v1, /device:TPU:1, one launch (start us, length us, event | category | flops | bytes accessed | tf_op | source)
XLA Modules:
  0.0 37.7 jit_solution(4726881377859024458)
XLA Ops:
  0.6 0.8 %pad_add_fusion.packed = f32[56,128]{1,0:T(8,128)S(1)} fusion(f32[2,96]{1,0:T(2,128)} %bitcast.16, f32[4,96]{1,0:T(4,128)} %bitcast.15, f32[2,96]{1,0:T(2,128)} %bitcast.17, f32[32,96]{1,0:T(8,128)} %bitcast.14), kind=kLoop, calls=%fused_computation | loop fusion | flops 21504 | bytes 44032 | tf_op jit(solution)/shard_map/add | solution.py:338
  1.4 34.5 %shard_map.84 = f32[56,128]{1,0:T(8,128)S(1)} custom-call(bf16[32,128,1024]{2,1,0:T(8,128)(2,1)} %bitcast.13, f32[56,128]{1,0:T(8,128)S(1)} %pad_add_fusion.packed), custom_call_target="tpu_custom_call" | custom-call | flops 1610612736 | bytes 8388608 | tf_op jit(solution)/shard_map/pallas_call | solution.py:339
  35.9 0.6 %slice_bitcast_fusion.1 = f32[96,4]{0,1:T(4,128)} fusion(f32[56,128]{1,0:T(8,128)S(1)} %shard_map.84), kind=kLoop, calls=%fused_computation.2 | loop fusion | bytes 3072 | tf_op jit(solution)/shard_map/transpose | solution.py:396
  36.5 0.6 %slice_bitcast_fusion.2 = (f32[96,2]{0,1:T(2,128)}, f32[96,2]{0,1:T(2,128)}) fusion(f32[56,128]{1,0:T(8,128)S(1)} %shard_map.84), kind=kLoop, calls=%fused_computation.3 | loop fusion | bytes 3072 | tf_op jit(solution)/shard_map/transpose | solution.py:396
  37.1 0.6 %slice_bitcast_fusion = f32[96,32]{0,1:T(8,128)} fusion(f32[56,128]{1,0:T(8,128)S(1)} %shard_map.84), kind=kLoop, calls=%fused_computation.1 | loop fusion | bytes 24576 | tf_op jit(solution)/shard_map/transpose | solution.py:396

commit v2 on v1

--- a/solution.py
+++ b/solution.py
@@ -20,15 +20,16 @@
 CHUNKS = 2
 CHUNK = COLS // CHUNKS
 PER = NLZ // CHUNKS
+PERQ = NLZ // 4
 LOADS = 8
 MSG = CW + 8
 QROWS = ROWS // 4
 
 (
-    S_ROW, S_BAND, S_BANDX, S_COL, S_COLC, S_R1, S_R2, S_R3, S_F1, S_F2,
-    S_GRAM, S_GRAMP, S_ROWS, S_BANDS,
-) = [0, 1, 2, 3, 4, 5, 7, 8, 9, 10, 11, 12, 13, 14]
-N_SEMS = 15
+    S_ROW, S_ROWC, S_BAND, S_COL, S_COLC, S_R1, S_R2, S_R3, S_F2,
+    S_GRAM, S_GRAMP, S_T1, S_ROWS, S_BANDS,
+) = [0, 1, 2, 3, 4, 5, 7, 8, 9, 10, 11, 12, 16, 17]
+N_SEMS = 18
 
 
 def dot(x, y):
@@ -75,11 +76,11 @@
 def kernel(
     tensor, packed,
     out,
-    data, mine4, mine2, rowg, bandg, bandx, row_t, band_t, bandx_t, tb_t,
+    data, mine2, rowg, bandg, row_t, band_t, bandx_t, tb_t,
     turned, prod, by_frame, part, recv1, sum1, recv2, fin, recv3,
     colg, colf, low, folded, partials,
-    fpart, fg, fsum, fx, gpart, grecv, gall, gcols,
-    rsend, rrecv, bsend, brecv,
+    fpart, fsum, fx, gpart, grecv, gall, gcols,
+    rsend, rcore, rsum, rrecv, bsend, brecv,
     local_sems, send_sems, recv_sems,
 ):
     a = lax.axis_index("gx")
@@ -91,7 +92,6 @@
     p = l * 2 + c
     other = 1 - c
     partner = lz * 2 + other
-    gy_peers = [wrap(g + k, NY) for k in range(1, NY)]
     gx_peers = [wrap(a + k, NX) for k in range(1, NX)]
     core_peers = [wrap(lz + k, NLZ) * 2 + c for k in range(1, NLZ)]
 
@@ -108,7 +108,7 @@
         pltpu.make_async_copy(ref, ref, send_sems.at[sem]).wait()
 
     barrier = pltpu.get_barrier_semaphore()
-    for to in gy_peers:
+    for to in core_peers + [partner, (lz + 8 - 16 * l) * 2 + other]:
         pl.semaphore_signal(barrier, inc=1, device_id=(a, to), device_id_type=MESH)
     for to in gx_peers:
         pl.semaphore_signal(barrier, inc=1, device_id=(to, g), device_id_type=MESH)
@@ -119,24 +119,18 @@
 
     tb_t[...] = jnp.zeros_like(tb_t)
     mine2[...] = packed[CW : CW + BW]
-    mine4[...] = packed[MSG : MSG + RW]
     time8 = packed[MSG + 8 :]
-    rowg[g] = mine4[...]
+    rowg[c, lz] = packed[MSG : MSG + 8]
     bandg[a] = mine2[...]
-    bandx[g] = mine2[...]
     for m, tile in enumerate(pack([packed[8 * m : 8 * m + 8] for m in range(4)])):
         colg[c, lz, 8 * m : 8 * m + 8] = tile
 
-    pl.semaphore_wait(barrier, NY - 1 + NX - 1)
-
-    for to in gy_peers:
-        send(mine4, rowg.at[g], S_ROW, (a, to))
+    pl.semaphore_wait(barrier, NLZ + 1 + NX - 1)
+
+    for to in core_peers:
+        send(rowg.at[c, lz], rowg.at[c, lz], S_ROW, (a, to))
     for to in gx_peers:
         send(mine2, bandg.at[a], S_BAND, (to, g))
-    for to in core_peers:
-        send(colg.at[c, lz], colg.at[c, lz], S_COL, (a, to))
-    for to in gy_peers:
-        send(mine2, bandx.at[g], S_BANDX, (a, to))
 
     @pl.loop(0, LOADS)
     def _(k):
@@ -147,15 +141,23 @@
             at = pl.multiple_of((k * per + i) * ROWS, ROWS)
             turned[:, pl.ds(at, ROWS)] = data[k * per + i].T
 
+        @pl.when(k == 0)
+        def _():
+            for to in core_peers:
+                send(colg.at[c, lz], colg.at[c, lz], S_COL, (a, to))
+
+    arrived(rowg.at[0, pl.ds(0, NLZ - 1)], S_ROW)
+    send(rowg.at[c], rowg.at[c], S_ROWC, (a, partner))
     arrived(bandg.at[pl.ds(0, NX - 1)], S_BAND)
     for k in range(NX):
         band_t[BW * k : BW * k + BW] = bandg[k]
     for t in range(FRAMES):
         tb_t[t * BANDS : (t + 1) * BANDS] = time8[t : t + 1] * band_t[...]
     tb_t[TB : TB + BANDS] = band_t[...]
-    arrived(rowg.at[pl.ds(0, NY - 1)], S_ROW)
+    arrived(rowg.at[0], S_ROWC)
     for k in range(NY):
-        row_t[RW * k : RW * k + RW] = rowg[k]
+        row_t[RW * k : RW * k + RW] = rowg[k % 2, k // 2, 0:RW]
+        bandx_t[RW * k : RW * k + RW] = rowg[k % 2, k // 2, RW : 2 * RW]
 
     @pl.loop(0, BANDS)
     def _(k):
@@ -200,9 +202,6 @@
     arrived(colg.at[0, pl.ds(0, NLZ - 1)], S_COL)
     send(colg.at[c], colg.at[c], S_COLC, (a, partner))
 
-    arrived(bandx.at[pl.ds(0, NY - 1)], S_BANDX)
-    for k in range(NY):
-        bandx_t[BW * k : BW * k + BW] = bandx[k]
     for i, ref in enumerate((row_t, bandx_t)):
         gram = exact(ref[...].T, ref[...])
         for k in range(4):
@@ -223,13 +222,22 @@
             colf[at : at + CW] = block
             low[at : at + CW] = block.astype(BF16)
 
+    fpart[...] = jnp.zeros_like(fpart)
     for t in range(FRAMES):
         fpart[t : t + 1] = jnp.sum(
             by_frame[t] * low[...].astype(F32), axis=0, keepdims=True
         )
-    fg[g] = fpart[...]
-    for to in gy_peers:
-        send(fpart, fg.at[g], S_F1, (a, to))
+
+    def send_rows(q):
+        span = pl.ds(q * PERQ, PERQ)
+        arrived(rcore.at[span], S_T1 + q)
+        rsum[span] = rsend[c, span] + rcore[span]
+        for i in range(PERQ):
+            k = q * PERQ + i
+
+            @pl.when(k != lz)
+            def _():
+                send(rsum.at[k], rrecv.at[lz], S_ROWS, (a, k * 2 + c))
 
     @pl.loop(0, 4)
     def _(q):
@@ -242,14 +250,16 @@
             rows = rows + block * tb_t[j : j + 1]
             block = block * row_here
             partials[q, j] = jnp.sum(block.reshape(QROWS // 8, 8, LANES), axis=0)
+        frames = fpart[...]
         for i in range(NY // 4):
-            rsend[q * (NY // 4) + i] = rows[RW * i : RW * i + RW]
-        for i in range(NY // 4):
-            k = q * (NY // 4) + i
-
-            @pl.when(k != g)
-            def _():
-                send(rsend.at[k], rrecv.at[g], S_ROWS, (a, k))
+            rsend[i % 2, q * PERQ + i // 2, 0:RW] = rows[RW * i : RW * i + RW]
+            rsend[i % 2, q * PERQ + i // 2, RW : 2 * RW] = frames
+        span = pl.ds(q * PERQ, PERQ)
+        send(rsend.at[other, span], rcore.at[span], S_T1 + q, (a, partner))
+
+        @pl.when(q > 0)
+        def _():
+            send_rows(q - 1)
 
     sums = total(partials, 4)
     bands = jnp.zeros((BANDS, LANES), F32)
@@ -261,7 +271,6 @@
         to = wrap(a + k, NX)
         send(bsend.at[to], brecv.at[a], S_BANDS, (to, g))
     brecv[a] = bsend[a]
-    rrecv[g] = rsend[g]
 
     arrived(grecv.at[pl.ds(0, NX - 1)], S_GRAM)
     gall[p] = total(grecv, NX)
@@ -269,11 +278,8 @@
         to = wrap(p + k, 4)
         to_l = lax.div(to, 2)
         send(gall.at[p], gall.at[p], S_GRAMP, (a, (to_l * 8 + z) * 2 + to - 2 * to_l))
-    arrived(fg.at[pl.ds(0, NY - 1)], S_F1)
-    fsum[...] = total(fg, NY)
-    fx[a] = fsum[...]
-    for to in gx_peers:
-        send(fsum, fx.at[a], S_F2, (to, g))
+    send_rows(3)
+    rrecv[lz] = rsum[lz]
     recv2[lz] = sum1[lz]
     arrived(recv2.at[pl.ds(0, NLZ - 1)], S_R2)
     fin[...] = total(recv2, NLZ)
@@ -287,6 +293,13 @@
     def _(i):
         block = colf[pl.ds(pl.multiple_of(i * 256, 256), 256)]
         gcols[...] += exact(block.T, block)
+
+    arrived(rrecv.at[pl.ds(0, NLZ - 1)], S_ROWS)
+    row_sums = total(rrecv, NLZ)
+    fsum[...] = row_sums[RW : RW + FRAMES]
+    fx[a] = fsum[...]
+    for to in gx_peers:
+        send(fsum, fx.at[a], S_F2, (to, g))
 
     gram_cols = gcols[...]
     arrived(gall.at[pl.ds(0, 3)], S_GRAMP)
@@ -301,38 +314,39 @@
     band_model = exact(packed[CW:MSG], gram_rows * gram_cols * gram_time)
     time_model = exact(time8, gram_rows * gram_cols * gram_bands)
 
-    arrived(fx.at[pl.ds(0, NX - 1)], S_F2)
-    out[CW : CW + FRAMES] = time_model[0:FRAMES] - total(fx, NX)
+    out[CW + 8 : CW + 8 + RW] = row_model[0:RW] - row_sums[0:RW]
     arrived(recv3.at[pl.ds(0, NX - 1)], S_R3)
     sums = total(recv3, NX)
     sums = jnp.concatenate(unpack([sums[8 * m : 8 * m + 8] for m in range(3)]), axis=0)
     out[0:CW] = col_model - sums
-    arrived(rrecv.at[pl.ds(0, NY - 1)], S_ROWS)
-    out[CW + 8 : CW + 8 + RW] = row_model[0:RW] - total(rrecv, NY)
     arrived(brecv.at[pl.ds(0, NX - 1)], S_BANDS)
     out[CW + 16 : CW + 16 + BW] = band_model[0:BW] - total(brecv, NX)
-
-    sent(rowg.at[pl.ds(0, NY - 1)], S_ROW)
+    arrived(fx.at[pl.ds(0, NX - 1)], S_F2)
+    out[CW : CW + FRAMES] = time_model[0:FRAMES] - total(fx, NX)
+
+    sent(rowg.at[0, pl.ds(0, NLZ - 1)], S_ROW)
+    sent(rowg.at[0], S_ROWC)
     sent(bandg.at[pl.ds(0, NX - 1)], S_BAND)
-    sent(bandx.at[pl.ds(0, NY - 1)], S_BANDX)
     sent(colg.at[0, pl.ds(0, NLZ - 1)], S_COL)
     sent(colg.at[0], S_COLC)
     for n in range(CHUNKS):
         sent(recv1.at[pl.ds(n * PER, PER)], S_R1 + n)
     sent(recv2.at[pl.ds(0, NLZ - 1)], S_R2)
     sent(recv3.at[pl.ds(0, NX - 1)], S_R3)
-    sent(fg.at[pl.ds(0, NY - 1)], S_F1)
     sent(fx.at[pl.ds(0, NX - 1)], S_F2)
     sent(grecv.at[pl.ds(0, NX - 1)], S_GRAM)
     sent(gall.at[pl.ds(0, 3)], S_GRAMP)
-    sent(rrecv.at[pl.ds(0, NY - 1)], S_ROWS)
+    for q in range(4):
+        sent(rcore.at[pl.ds(q * PERQ, PERQ)], S_T1 + q)
+    sent(rrecv.at[pl.ds(0, NLZ - 1)], S_ROWS)
     sent(brecv.at[pl.ds(0, NX - 1)], S_BANDS)
 
 
 def shards(tensor, row_factor, column_factor, band_factor, time_factor):
     v = pltpu.VMEM
     packed = jnp.zeros((MSG + 16, LANES), F32)
-    pieces = ((0, column_factor), (CW, band_factor), (MSG, row_factor), (MSG + 8, time_factor))
+    pieces = ((0, column_factor), (CW, band_factor), (MSG, row_factor))
+    pieces += ((MSG + RW, band_factor), (MSG + 8, time_factor))
     for at, x in pieces:
         x = x.T
         packed = packed + jnp.pad(x, ((at, MSG + 16 - at - x.shape[0]), (0, LANES - RANK)))
@@ -343,14 +357,12 @@
         out_specs=pl.BlockSpec(memory_space=v),
         scratch_shapes=[
             v((TB, ROWS, COLS), BF16),
-            v((RW, LANES), F32),
             v((BW, LANES), F32),
-            v((NY, RW, LANES), F32),
+            v((2, NLZ, 8, LANES), F32),
             v((NX, BW, LANES), F32),
-            v((NY, BW, LANES), F32),
             v((ROWS, LANES), F32),
             v((BANDS, LANES), F32),
-            v((NY * BW, LANES), F32),
+            v((NY * RW, LANES), F32),
             v((LANES, LANES), F32),
             v((COLS, TB * ROWS), BF16),
             v((FRAMES, HALF, 2 * LANES), BF16),
@@ -366,16 +378,17 @@
             v((COLS, LANES), BF16),
             v((TB * QROWS, LANES), F32),
             v((4, TB, 8, LANES), F32),
-            v((FRAMES, LANES), F32),
-            v((NY, FRAMES, LANES), F32),
+            v((RW, LANES), F32),
             v((FRAMES, LANES), F32),
             v((NX, FRAMES, LANES), F32),
             v((4, 2, 24, LANES), F32),
             v((NX, 2, 24, LANES), F32),
             v((4, 2, 24, LANES), F32),
             v((LANES, LANES), F32),
-            v((NY, RW, LANES), F32),
-            v((NY, RW, LANES), F32),
+            v((2, NLZ, 8, LANES), F32),
+            v((NLZ, 8, LANES), F32),
+            v((NLZ, 8, LANES), F32),
+            v((NLZ, 8, LANES), F32),
             v((NX, BW, LANES), F32),
             v((NX, BW, LANES), F32),
             pltpu.SemaphoreType.DMA((LOADS,)),

time: 37.9 us -> 37.7 us (level)
  no operation moved by 1% of the time
where the time goes in v2:
time: 37.7 us; the launch traced here: 37.5 us
  Pallas kernels  34.3 us (91%)
  local copies, waits for them, and re-layouts  1.75 us (5%)
  other arithmetic  0.79 us (2%)
  between operations  0.64 us (2%)
    pallas_call x1, Pallas kernels, shards(): pl.pallas_call(kernel, out_shape=jax.ShapeDtypeStruct((CW + 24, LANES), F...  34.3 us
    transpose x3, local copies, waits for them, and re-layouts, shards(): return tuple((out[at:at + n, 0:RANK].T for at, n in places))  1.75 us
    add x1, other arithmetic, shards(): packed + jnp.pad(x, ((at, MSG + 16 - at - x.shape[0]), (0, LANES - RANK)))  0.79 us

profile of v2, /device:TPU:1, one launch (start us, length us, event | category | flops | bytes accessed | tf_op | source)
XLA Modules:
  0.0 37.5 jit_solution(17776700731254558422)
XLA Ops:
  0.6 0.8 %pad_add_fusion.packed = f32[56,128]{1,0:T(8,128)S(1)} fusion(f32[2,96]{1,0:T(2,128)} %bitcast.16, f32[2,96]{1,0:T(2,128)} %bitcast.17, f32[4,96]{1,0:T(4,128)} %bitcast.15, f32[32,96]{1,0:T(8,128)} %bitcast.14), kind=kLoop, calls=%fused_computation | loop fusion | flops 28672 | bytes 44032 | tf_op jit(solution)/shard_map/add | solution.py:352
  1.4 34.3 %shard_map.84 = f32[56,128]{1,0:T(8,128)S(1)} custom-call(bf16[32,128,1024]{2,1,0:T(8,128)(2,1)} %bitcast.13, f32[56,128]{1,0:T(8,128)S(1)} %pad_add_fusion.packed), custom_call_target="tpu_custom_call" | custom-call | flops 1610612736 | bytes 8388608 | tf_op jit(solution)/shard_map/pallas_call | solution.py:353
  35.8 0.6 %slice_bitcast_fusion.1 = f32[96,4]{0,1:T(4,128)} fusion(f32[56,128]{1,0:T(8,128)S(1)} %shard_map.84), kind=kLoop, calls=%fused_computation.2 | loop fusion | bytes 3072 | tf_op jit(solution)/shard_map/transpose | solution.py:409
  36.3 0.6 %slice_bitcast_fusion.2 = (f32[96,2]{0,1:T(2,128)}, f32[96,2]{0,1:T(2,128)}) fusion(f32[56,128]{1,0:T(8,128)S(1)} %shard_map.84), kind=kLoop, calls=%fused_computation.3 | loop fusion | bytes 3072 | tf_op jit(solution)/shard_map/transpose | solution.py:409
  36.9 0.6 %slice_bitcast_fusion = f32[96,32]{0,1:T(8,128)} fusion(f32[56,128]{1,0:T(8,128)S(1)} %shard_map.84), kind=kLoop, calls=%fused_computation.1 | loop fusion | bytes 24576 | tf_op jit(solution)/shard_map/transpose | solution.py:409

commit v3 on v1

--- a/solution.py
+++ b/solution.py
@@ -133,10 +133,6 @@
         send(mine4, rowg.at[g], S_ROW, (a, to))
     for to in gx_peers:
         send(mine2, bandg.at[a], S_BAND, (to, g))
-    for to in core_peers:
-        send(colg.at[c, lz], colg.at[c, lz], S_COL, (a, to))
-    for to in gy_peers:
-        send(mine2, bandx.at[g], S_BANDX, (a, to))
 
     @pl.loop(0, LOADS)
     def _(k):
@@ -146,6 +142,11 @@
         for i in range(per):
             at = pl.multiple_of((k * per + i) * ROWS, ROWS)
             turned[:, pl.ds(at, ROWS)] = data[k * per + i].T
+
+    for to in core_peers:
+        send(colg.at[c, lz], colg.at[c, lz], S_COL, (a, to))
+    for to in gy_peers:
+        send(mine2, bandx.at[g], S_BANDX, (a, to))
 
     arrived(bandg.at[pl.ds(0, NX - 1)], S_BAND)
     for k in range(NX):
@@ -197,18 +198,19 @@
         def _():
             send_pieces(n - 1)
 
+    gram = exact(row_t[...].T, row_t[...])
+    for k in range(4):
+        gpart[k, 0] = gram[24 * k : 24 * k + 24]
+    send_pieces(CHUNKS - 1)
     arrived(colg.at[0, pl.ds(0, NLZ - 1)], S_COL)
     send(colg.at[c], colg.at[c], S_COLC, (a, partner))
-
     arrived(bandx.at[pl.ds(0, NY - 1)], S_BANDX)
     for k in range(NY):
         bandx_t[BW * k : BW * k + BW] = bandx[k]
-    for i, ref in enumerate((row_t, bandx_t)):
-        gram = exact(ref[...].T, ref[...])
-        for k in range(4):
-            gpart[k, i] = gram[24 * k : 24 * k + 24]
+    gram = exact(bandx_t[...].T, bandx_t[...])
+    for k in range(4):
+        gpart[k, 1] = gram[24 * k : 24 * k + 24]
     grecv[a] = gpart[p]
-    send_pieces(CHUNKS - 1)
     for to in gx_peers:
         send(gpart.at[p], grecv.at[a], S_GRAM, (to, g))
 

time: 37.9 us -> 38.5 us (1.016)
  Pallas kernels: 34.5 us -> 35.1 us
    pallas_call x1, Pallas kernels: 34.5 us -> 35.1 us  [shards(): pl.pallas_call(kernel, out_shape=jax.ShapeDtypeStruct((CW + 24, LANES), F...]
where the time goes in v3:
time: 38.5 us; the launch traced here: 38.3 us
  Pallas kernels  35.1 us (91%)
  local copies, waits for them, and re-layouts  1.75 us (5%)
  other arithmetic  0.77 us (2%)
  between operations  0.64 us (2%)
    pallas_call x1, Pallas kernels, shards(): pl.pallas_call(kernel, out_shape=jax.ShapeDtypeStruct((CW + 24, LANES), F...  35.1 us
    transpose x3, local copies, waits for them, and re-layouts, shards(): return tuple((out[at:at + n, 0:RANK].T for at, n in places))  1.75 us
    add x1, other arithmetic, shards(): packed + jnp.pad(x, ((at, MSG + 16 - at - x.shape[0]), (0, LANES - RANK)))  0.77 us

profile of v3, /device:TPU:1, one launch (start us, length us, event | category | flops | bytes accessed | tf_op | source)
XLA Modules:
  0.0 38.3 jit_solution(8801709709604097857)
XLA Ops:
  0.6 0.8 %pad_add_fusion.packed = f32[56,128]{1,0:T(8,128)S(1)} fusion(f32[2,96]{1,0:T(2,128)} %bitcast.16, f32[4,96]{1,0:T(4,128)} %bitcast.15, f32[2,96]{1,0:T(2,128)} %bitcast.17, f32[32,96]{1,0:T(8,128)} %bitcast.14), kind=kLoop, calls=%fused_computation | loop fusion | flops 21504 | bytes 44032 | tf_op jit(solution)/shard_map/add | solution.py:340
  1.4 35.1 %shard_map.84 = f32[56,128]{1,0:T(8,128)S(1)} custom-call(bf16[32,128,1024]{2,1,0:T(8,128)(2,1)} %bitcast.13, f32[56,128]{1,0:T(8,128)S(1)} %pad_add_fusion.packed), custom_call_target="tpu_custom_call" | custom-call | flops 1610612736 | bytes 8388608 | tf_op jit(solution)/shard_map/pallas_call | solution.py:341
  36.5 0.6 %slice_bitcast_fusion.1 = f32[96,4]{0,1:T(4,128)} fusion(f32[56,128]{1,0:T(8,128)S(1)} %shard_map.84), kind=kLoop, calls=%fused_computation.2 | loop fusion | bytes 3072 | tf_op jit(solution)/shard_map/transpose | solution.py:398
  37.1 0.6 %slice_bitcast_fusion.2 = (f32[96,2]{0,1:T(2,128)}, f32[96,2]{0,1:T(2,128)}) fusion(f32[56,128]{1,0:T(8,128)S(1)} %shard_map.84), kind=kLoop, calls=%fused_computation.3 | loop fusion | bytes 3072 | tf_op jit(solution)/shard_map/transpose | solution.py:398
  37.7 0.6 %slice_bitcast_fusion = f32[96,32]{0,1:T(8,128)} fusion(f32[56,128]{1,0:T(8,128)S(1)} %shard_map.84), kind=kLoop, calls=%fused_computation.1 | loop fusion | bytes 24576 | tf_op jit(solution)/shard_map/transpose | solution.py:398

commit v4 on v3

--- a/solution.py
+++ b/solution.py
@@ -17,7 +17,7 @@
 PACK = CW * RANK // LANES
 TB = FRAMES * BANDS
 HALF = BANDS * ROWS
-CHUNKS = 2
+CHUNKS = 4
 CHUNK = COLS // CHUNKS
 PER = NLZ // CHUNKS
 LOADS = 8
@@ -27,8 +27,8 @@
 (
     S_ROW, S_BAND, S_BANDX, S_COL, S_COLC, S_R1, S_R2, S_R3, S_F1, S_F2,
     S_GRAM, S_GRAMP, S_ROWS, S_BANDS,
-) = [0, 1, 2, 3, 4, 5, 7, 8, 9, 10, 11, 12, 13, 14]
-N_SEMS = 15
+) = [0, 1, 2, 3, 4, 5, 9, 10, 11, 12, 13, 14, 15, 16]
+N_SEMS = 17
 
 
 def dot(x, y):
@@ -73,8 +73,9 @@
 
 
 def kernel(
-    tensor, packed,
-    out,
+    tensor, row_in, col_in, band_in, time_in,
+    row_out, col_out, band_out, time_out,
+    packed, row_v, col_v, band_v, time_v,
     data, mine4, mine2, rowg, bandg, bandx, row_t, band_t, bandx_t, tb_t,
     turned, prod, by_frame, part, recv1, sum1, recv2, fin, recv3,
     colg, colf, low, folded, partials,
@@ -107,6 +108,15 @@
     def sent(ref, sem):
         pltpu.make_async_copy(ref, ref, send_sems.at[sem]).wait()
 
+    small = [
+        pltpu.make_async_copy(src, dst, local_sems.at[LOADS + k])
+        for k, (src, dst) in enumerate(
+            [(row_in, row_v), (band_in, band_v), (col_in, col_v), (time_in, time_v)]
+        )
+    ]
+    for copy in small:
+        copy.start()
+
     barrier = pltpu.get_barrier_semaphore()
     for to in gy_peers:
         pl.semaphore_signal(barrier, inc=1, device_id=(a, to), device_id_type=MESH)
@@ -118,6 +128,13 @@
         pltpu.make_async_copy(tensor.at[span], data.at[span], local_sems.at[k]).start()
 
     tb_t[...] = jnp.zeros_like(tb_t)
+    packed[...] = jnp.zeros_like(packed)
+    for copy in small:
+        copy.wait()
+    packed[0:CW, 0:RANK] = col_v[...]
+    packed[CW : CW + BW, 0:RANK] = band_v[...]
+    packed[MSG : MSG + RW, 0:RANK] = row_v[...]
+    packed[MSG + 8 : MSG + 8 + FRAMES, 0:RANK] = time_v[...]
     mine2[...] = packed[CW : CW + BW]
     mine4[...] = packed[MSG : MSG + RW]
     time8 = packed[MSG + 8 :]
@@ -304,15 +321,15 @@
     time_model = exact(time8, gram_rows * gram_cols * gram_bands)
 
     arrived(fx.at[pl.ds(0, NX - 1)], S_F2)
-    out[CW : CW + FRAMES] = time_model[0:FRAMES] - total(fx, NX)
+    time_out[...] = (time_model[0:FRAMES] - total(fx, NX))[:, 0:RANK]
     arrived(recv3.at[pl.ds(0, NX - 1)], S_R3)
     sums = total(recv3, NX)
     sums = jnp.concatenate(unpack([sums[8 * m : 8 * m + 8] for m in range(3)]), axis=0)
-    out[0:CW] = col_model - sums
+    col_out[...] = (col_model - sums)[:, 0:RANK]
     arrived(rrecv.at[pl.ds(0, NY - 1)], S_ROWS)
-    out[CW + 8 : CW + 8 + RW] = row_model[0:RW] - total(rrecv, NY)
+    row_out[...] = (row_model[0:RW] - total(rrecv, NY))[:, 0:RANK]
     arrived(brecv.at[pl.ds(0, NX - 1)], S_BANDS)
-    out[CW + 16 : CW + 16 + BW] = band_model[0:BW] - total(brecv, NX)
+    band_out[...] = (band_model[0:BW] - total(brecv, NX))[:, 0:RANK]
 
     sent(rowg.at[pl.ds(0, NY - 1)], S_ROW)
     sent(bandg.at[pl.ds(0, NX - 1)], S_BAND)
@@ -331,19 +348,33 @@
     sent(brecv.at[pl.ds(0, NX - 1)], S_BANDS)
 
 
+def hand_over(*refs):
+    sems = refs[8]
+    copies = [
+        pltpu.make_async_copy(refs[k], refs[4 + k], sems.at[k]) for k in range(4)
+    ]
+    for copy in copies:
+        copy.start()
+    for copy in copies:
+        copy.wait()
+
+
 def shards(tensor, row_factor, column_factor, band_factor, time_factor):
     v = pltpu.VMEM
-    packed = jnp.zeros((MSG + 16, LANES), F32)
-    pieces = ((0, column_factor), (CW, band_factor), (MSG, row_factor), (MSG + 8, time_factor))
-    for at, x in pieces:
-        x = x.T
-        packed = packed + jnp.pad(x, ((at, MSG + 16 - at - x.shape[0]), (0, LANES - RANK)))
+    shapes = tuple(jax.ShapeDtypeStruct((n, RANK), F32) for n in (RW, CW, BW, FRAMES))
+    factors = (row_factor, column_factor, band_factor, time_factor)
+    factors = [pltpu.with_memory_space_constraint(x.T, pltpu.HBM) for x in factors]
     out = pl.pallas_call(
         kernel,
-        out_shape=jax.ShapeDtypeStruct((CW + 24, LANES), F32),
-        in_specs=[pl.BlockSpec(memory_space=pl.ANY), pl.BlockSpec(memory_space=v)],
-        out_specs=pl.BlockSpec(memory_space=v),
+        out_shape=shapes,
+        in_specs=[pl.BlockSpec(memory_space=pl.ANY)] + [pl.BlockSpec(memory_space=pltpu.HBM)] * 4,
+        out_specs=[pl.BlockSpec(memory_space=v)] * 4,
         scratch_shapes=[
+            v((MSG + 16, LANES), F32),
+            v((RW, RANK), F32),
+            v((CW, RANK), F32),
+            v((BW, RANK), F32),
+            v((FRAMES, RANK), F32),
             v((TB, ROWS, COLS), BF16),
             v((RW, LANES), F32),
             v((BW, LANES), F32),
@@ -380,7 +411,7 @@
             v((NY, RW, LANES), F32),
             v((NX, BW, LANES), F32),
             v((NX, BW, LANES), F32),
-            pltpu.SemaphoreType.DMA((LOADS,)),
+            pltpu.SemaphoreType.DMA((LOADS + 4,)),
             pltpu.SemaphoreType.DMA((N_SEMS,)),
             pltpu.SemaphoreType.DMA((N_SEMS,)),
         ],
@@ -392,10 +423,16 @@
         ),
     )(
         tensor.reshape(TB, ROWS, COLS),
-        packed,
+        *factors,
     )
-    places = ((CW + 8, RW), (0, CW), (CW + 16, BW), (CW, FRAMES))
-    return tuple(out[at : at + n, 0:RANK].T for at, n in places)
+    out = pl.pallas_call(
+        hand_over,
+        out_shape=shapes,
+        in_specs=[pl.BlockSpec(memory_space=v)] * 4,
+        out_specs=[pl.BlockSpec(memory_space=pl.ANY)] * 4,
+        scratch_shapes=[pltpu.SemaphoreType.DMA((4,))],
+    )(*[pltpu.with_memory_space_constraint(x, v) for x in out])
+    return tuple(x.T for x in out)
 
 
 def solution(mesh):

time: 38.5 us -> 36.7 us (0.953)
  local copies, waits for them, and re-layouts: 1.75 us -> 0 us
  Pallas kernels: 35.1 us -> 36 us
  other arithmetic: 0.77 us -> 0 us
    transpose x3 -> x0, local copies, waits for them, and re-layouts: 1.75 us -> none  [shards(): return tuple((out[at:at + n, 0:RANK].T for at, n in places))]
    pallas_call x1 -> x2, Pallas kernels: 35.1 us -> 36 us  [the longest x1 35.3 us: shards(): pl.pallas_call(kernel, out_shape=shapes, in_specs=[pl.BlockSpec(memory_sp...]
    add x1 -> x0, other arithmetic: 0.77 us -> none  [shards(): packed + jnp.pad(x, ((at, MSG + 16 - at - x.shape[0]), (0, LANES - RANK)))]
where the time goes in v4:
time: 36.7 us; the launch traced here: 36.6 us
  Pallas kernels  36 us (98%)
  between operations  0.64 us (2%)
    pallas_call x1, Pallas kernels, shards(): pl.pallas_call(kernel, out_shape=shapes, in_specs=[pl.BlockSpec(memory_sp...  35.3 us

profile of v4, /device:TPU:1, one launch (start us, length us, event | category | flops | bytes accessed | tf_op | source)
XLA Modules:
  0.0 36.6 jit_solution(1382897598410691478)
XLA Ops:
  0.6 35.3 %shard_map.84 = (f32[4,96]{1,0:T(4,128)S(1)}, f32[32,96]{1,0:T(8,128)S(1)}, f32[2,96]{1,0:T(2,128)S(1)}, f32[2,96]{1,0:T(2,128)S(1)}) custom-call(bf16[32,128,1024]{2,1,0:T(8,128)(2,1)} %bitcast.9, f32[4,96]{1,0:T(4,128)} %bitcast.11, f32[32,96]{1,0:T(8,128)} %bitcast.10, f32[2,96]{1,0:T(2,128)} %bitcast.12, f32[2,96]{1,0:T(2,128)} %bitcast.13), custom_call_target="tpu_custom_call" | custom-call | flops 1610612736 | bytes 8388608 | tf_op jit(solution)/shard_map/pallas_call | solution.py:367
  35.9 0.7 %shard_map.85 = (f32[4,96]{1,0:T(4,128)}, f32[32,96]{1,0:T(8,128)}, f32[2,96]{1,0:T(2,128)}, f32[2,96]{1,0:T(2,128)}) custom-call(f32[4,96]{1,0:T(4,128)S(1)} %get-tuple-element.12.refs_0_, f32[32,96]{1,0:T(8,128)S(1)} %get-tuple-element.13.refs_1_, f32[2,96]{1,0:T(2,128)S(1)} %get-tuple-element.14.refs_2_, f32[2,96]{1,0:T(2,128)S(1)} %get-tuple-element.15.refs_3_), custom_call_target="tpu_custom_call" | custom-call | tf_op jit(solution)/shard_map/pallas_call | solution.py:428

commit v5 on v4

--- a/solution.py
+++ b/solution.py
@@ -150,6 +150,8 @@
         send(mine4, rowg.at[g], S_ROW, (a, to))
     for to in gx_peers:
         send(mine2, bandg.at[a], S_BAND, (to, g))
+    for to in core_peers:
+        send(colg.at[c, lz], colg.at[c, lz], S_COL, (a, to))
 
     @pl.loop(0, LOADS)
     def _(k):
@@ -160,8 +162,6 @@
             at = pl.multiple_of((k * per + i) * ROWS, ROWS)
             turned[:, pl.ds(at, ROWS)] = data[k * per + i].T
 
-    for to in core_peers:
-        send(colg.at[c, lz], colg.at[c, lz], S_COL, (a, to))
     for to in gy_peers:
         send(mine2, bandx.at[g], S_BANDX, (a, to))
 
@@ -184,24 +184,40 @@
             prod[t, span, 0:LANES] = (tb_t[pl.ds(t * BANDS + k, 1)] * rows).astype(BF16)
             prod[t, span, LANES:] = plain
 
+    def slot_lz(n, i):
+        return (i // 2) * (NLZ // 2) + 2 * n + i % 2
+
     def send_pieces(n):
         span = pl.ds(n * PER, PER)
         arrived(recv1.at[span], S_R1 + n)
         sum1[span] = part[c, span] + recv1[span]
         for i in range(PER):
-            k = n * PER + i
+            k = slot_lz(n, i)
 
             @pl.when(k != lz)
             def _():
-                send(sum1.at[k], recv2.at[lz], S_R2, (a, k * 2 + c))
+                send(sum1.at[n * PER + i], recv2.at[lz], S_R2, (a, k * 2 + c))
+
+            @pl.when(k == lz)
+            def _():
+                recv2[lz] = sum1[n * PER + i]
 
     @pl.loop(0, CHUNKS)
     def _(n):
-        here = pl.ds(pl.multiple_of(n * CHUNK, CHUNK), CHUNK)
+        heres = [
+            pl.ds(pl.multiple_of(i * (COLS // 2) + n * (CHUNK // 2), CHUNK // 2), CHUNK // 2)
+            for i in range(2)
+        ]
         acc = jnp.zeros((CHUNK, LANES), F32)
         for t in range(FRAMES):
-            both = dot(turned[here, t * HALF : (t + 1) * HALF], prod[t])
-            by_frame[t, here] = both[:, LANES:]
+            both = dot(
+                jnp.concatenate(
+                    [turned[here, t * HALF : (t + 1) * HALF] for here in heres], axis=0
+                ),
+                prod[t],
+            )
+            for i, here in enumerate(heres):
+                by_frame[t, here] = both[i * (CHUNK // 2) : (i + 1) * (CHUNK // 2), LANES:]
             acc = acc + both[:, 0:LANES]
         acc = acc.reshape(CHUNK // CW, 4, 8, LANES)
         tiles = pack([acc[:, m].reshape(CHUNK // 4, LANES) for m in range(4)])
@@ -211,14 +227,14 @@
         span = pl.ds(n * PER, PER)
         send(part.at[other, span], recv1.at[span], S_R1 + n, (a, partner))
 
-        @pl.when(n > 0)
-        def _():
-            send_pieces(n - 1)
-
     gram = exact(row_t[...].T, row_t[...])
     for k in range(4):
         gpart[k, 0] = gram[24 * k : 24 * k + 24]
-    send_pieces(CHUNKS - 1)
+
+    @pl.loop(0, CHUNKS)
+    def _(n):
+        send_pieces(n)
+
     arrived(colg.at[0, pl.ds(0, NLZ - 1)], S_COL)
     send(colg.at[c], colg.at[c], S_COLC, (a, partner))
     arrived(bandx.at[pl.ds(0, NY - 1)], S_BANDX)
@@ -252,19 +268,21 @@
 
     @pl.loop(0, 4)
     def _(q):
-        here = pl.ds(pl.multiple_of(q * QROWS, QROWS), QROWS)
-        folded[...] = dot(data[:, here, :].reshape(TB * QROWS, COLS), low[...])
+        half = QROWS // 2
+        heres = [pl.ds(pl.multiple_of(i * (ROWS // 2) + q * half, half), half) for i in range(2)]
+        block = jnp.concatenate([data[:, here, :] for here in heres], axis=1)
+        folded[...] = dot(block.reshape(TB * QROWS, COLS), low[...])
         rows = jnp.zeros((QROWS, LANES), F32)
-        row_here = row_t[here]
+        row_here = jnp.concatenate([row_t[here] for here in heres], axis=0)
         for j in range(TB):
             block = folded[j * QROWS : (j + 1) * QROWS]
             rows = rows + block * tb_t[j : j + 1]
             block = block * row_here
             partials[q, j] = jnp.sum(block.reshape(QROWS // 8, 8, LANES), axis=0)
-        for i in range(NY // 4):
-            rsend[q * (NY // 4) + i] = rows[RW * i : RW * i + RW]
-        for i in range(NY // 4):
-            k = q * (NY // 4) + i
+        owners = [(i // 4) * (NY // 2) + 4 * q + i % 4 for i in range(NY // 4)]
+        for i, k in enumerate(owners):
+            rsend[k] = rows[RW * i : RW * i + RW]
+        for k in owners:
 
             @pl.when(k != g)
             def _():
@@ -288,17 +306,16 @@
         to = wrap(p + k, 4)
         to_l = lax.div(to, 2)
         send(gall.at[p], gall.at[p], S_GRAMP, (a, (to_l * 8 + z) * 2 + to - 2 * to_l))
+    arrived(recv2.at[pl.ds(0, NLZ - 1)], S_R2)
+    fin[...] = total(recv2, NLZ)
+    recv3[a] = fin[...]
+    for to in gx_peers:
+        send(fin, recv3.at[a], S_R3, (to, g))
     arrived(fg.at[pl.ds(0, NY - 1)], S_F1)
     fsum[...] = total(fg, NY)
     fx[a] = fsum[...]
     for to in gx_peers:
         send(fsum, fx.at[a], S_F2, (to, g))
-    recv2[lz] = sum1[lz]
-    arrived(recv2.at[pl.ds(0, NLZ - 1)], S_R2)
-    fin[...] = total(recv2, NLZ)
-    recv3[a] = fin[...]
-    for to in gx_peers:
-        send(fin, recv3.at[a], S_R3, (to, g))
 
     gcols[...] = jnp.zeros_like(gcols)
 

time: 36.7 us -> 36.5 us (level)
  no operation moved by 1% of the time
where the time goes in v5:
time: 36.5 us; the launch traced here: 36.4 us
  Pallas kernels  35.8 us (98%)
  between operations  0.64 us (2%)
    pallas_call x1, Pallas kernels, shards(): pl.pallas_call(kernel, out_shape=shapes, in_specs=[pl.BlockSpec(memory_sp...  35.1 us

profile of v5, /device:TPU:1, one launch (start us, length us, event | category | flops | bytes accessed | tf_op | source)
XLA Modules:
  0.0 36.4 jit_solution(16077101003526814189)
XLA Ops:
  0.6 35.1 %shard_map.84 = (f32[4,96]{1,0:T(4,128)S(1)}, f32[32,96]{1,0:T(8,128)S(1)}, f32[2,96]{1,0:T(2,128)S(1)}, f32[2,96]{1,0:T(2,128)S(1)}) custom-call(bf16[32,128,1024]{2,1,0:T(8,128)(2,1)} %bitcast.9, f32[4,96]{1,0:T(4,128)} %bitcast.11, f32[32,96]{1,0:T(8,128)} %bitcast.10, f32[2,96]{1,0:T(2,128)} %bitcast.12, f32[2,96]{1,0:T(2,128)} %bitcast.13), custom_call_target="tpu_custom_call" | custom-call | flops 1610612736 | bytes 8388608 | tf_op jit(solution)/shard_map/pallas_call | solution.py:384
  35.8 0.7 %shard_map.85 = (f32[4,96]{1,0:T(4,128)}, f32[32,96]{1,0:T(8,128)}, f32[2,96]{1,0:T(2,128)}, f32[2,96]{1,0:T(2,128)}) custom-call(f32[4,96]{1,0:T(4,128)S(1)} %get-tuple-element.12.refs_0_, f32[32,96]{1,0:T(8,128)S(1)} %get-tuple-element.13.refs_1_, f32[2,96]{1,0:T(2,128)S(1)} %get-tuple-element.14.refs_2_, f32[2,96]{1,0:T(2,128)S(1)} %get-tuple-element.15.refs_3_), custom_call_target="tpu_custom_call" | custom-call | tf_op jit(solution)/shard_map/pallas_call | solution.py:445

commit v6 on v5

--- a/solution.py
+++ b/solution.py
@@ -25,10 +25,10 @@
 QROWS = ROWS // 4
 
 (
-    S_ROW, S_BAND, S_BANDX, S_COL, S_COLC, S_R1, S_R2, S_R3, S_F1, S_F2,
-    S_GRAM, S_GRAMP, S_ROWS, S_BANDS,
-) = [0, 1, 2, 3, 4, 5, 9, 10, 11, 12, 13, 14, 15, 16]
-N_SEMS = 17
+    S_ROW, S_ROWC, S_BAND, S_COL, S_COLC, S_R1, S_R2, S_R3, S_F2,
+    S_GRAM, S_GRAMP, S_T1, S_ROWS,
+) = [0, 1, 2, 3, 4, 5, 9, 10, 11, 12, 13, 14, 18]
+N_SEMS = 19
 
 
 def dot(x, y):
@@ -76,11 +76,11 @@
     tensor, row_in, col_in, band_in, time_in,
     row_out, col_out, band_out, time_out,
     packed, row_v, col_v, band_v, time_v,
-    data, mine4, mine2, rowg, bandg, bandx, row_t, band_t, bandx_t, tb_t,
-    turned, prod, by_frame, part, recv1, sum1, recv2, fin, recv3,
+    data, mine2, rowg, bandg, row_t, band_t, bandx_t, tb_t,
+    turned, prod, by_frame, part, recv1, sum1, recv2, xsend, recv3,
     colg, colf, low, folded, partials,
-    fpart, fg, fsum, fx, gpart, grecv, gall, gcols,
-    rsend, rrecv, bsend, brecv,
+    fpart, fsum, fx, gpart, grecv, gall, gcols,
+    rsend, rcore, rsum, rrecv,
     local_sems, send_sems, recv_sems,
 ):
     a = lax.axis_index("gx")
@@ -92,7 +92,6 @@
     p = l * 2 + c
     other = 1 - c
     partner = lz * 2 + other
-    gy_peers = [wrap(g + k, NY) for k in range(1, NY)]
     gx_peers = [wrap(a + k, NX) for k in range(1, NX)]
     core_peers = [wrap(lz + k, NLZ) * 2 + c for k in range(1, NLZ)]
 
@@ -118,7 +117,7 @@
         copy.start()
 
     barrier = pltpu.get_barrier_semaphore()
-    for to in gy_peers:
+    for to in core_peers + [partner, (lz + 8 - 16 * l) * 2 + other]:
         pl.semaphore_signal(barrier, inc=1, device_id=(a, to), device_id_type=MESH)
     for to in gx_peers:
         pl.semaphore_signal(barrier, inc=1, device_id=(to, g), device_id_type=MESH)
@@ -134,20 +133,19 @@
     packed[0:CW, 0:RANK] = col_v[...]
     packed[CW : CW + BW, 0:RANK] = band_v[...]
     packed[MSG : MSG + RW, 0:RANK] = row_v[...]
+    packed[MSG + RW : MSG + RW + BW, 0:RANK] = band_v[...]
     packed[MSG + 8 : MSG + 8 + FRAMES, 0:RANK] = time_v[...]
     mine2[...] = packed[CW : CW + BW]
-    mine4[...] = packed[MSG : MSG + RW]
     time8 = packed[MSG + 8 :]
-    rowg[g] = mine4[...]
+    rowg[c, lz] = packed[MSG : MSG + 8]
     bandg[a] = mine2[...]
-    bandx[g] = mine2[...]
     for m, tile in enumerate(pack([packed[8 * m : 8 * m + 8] for m in range(4)])):
         colg[c, lz, 8 * m : 8 * m + 8] = tile
 
-    pl.semaphore_wait(barrier, NY - 1 + NX - 1)
-
-    for to in gy_peers:
-        send(mine4, rowg.at[g], S_ROW, (a, to))
+    pl.semaphore_wait(barrier, NLZ + 1 + NX - 1)
+
+    for to in core_peers:
+        send(rowg.at[c, lz], rowg.at[c, lz], S_ROW, (a, to))
     for to in gx_peers:
         send(mine2, bandg.at[a], S_BAND, (to, g))
     for to in core_peers:
@@ -162,18 +160,18 @@
             at = pl.multiple_of((k * per + i) * ROWS, ROWS)
             turned[:, pl.ds(at, ROWS)] = data[k * per + i].T
 
-    for to in gy_peers:
-        send(mine2, bandx.at[g], S_BANDX, (a, to))
-
+    arrived(rowg.at[0, pl.ds(0, NLZ - 1)], S_ROW)
+    send(rowg.at[c], rowg.at[c], S_ROWC, (a, partner))
     arrived(bandg.at[pl.ds(0, NX - 1)], S_BAND)
     for k in range(NX):
         band_t[BW * k : BW * k + BW] = bandg[k]
     for t in range(FRAMES):
         tb_t[t * BANDS : (t + 1) * BANDS] = time8[t : t + 1] * band_t[...]
     tb_t[TB : TB + BANDS] = band_t[...]
-    arrived(rowg.at[pl.ds(0, NY - 1)], S_ROW)
+    arrived(rowg.at[0], S_ROWC)
     for k in range(NY):
-        row_t[RW * k : RW * k + RW] = rowg[k]
+        row_t[RW * k : RW * k + RW] = rowg[k % 2, k // 2, 0:RW]
+        bandx_t[RW * k : RW * k + RW] = rowg[k % 2, k // 2, RW : 2 * RW]
 
     @pl.loop(0, BANDS)
     def _(k):
@@ -227,25 +225,19 @@
         span = pl.ds(n * PER, PER)
         send(part.at[other, span], recv1.at[span], S_R1 + n, (a, partner))
 
-    gram = exact(row_t[...].T, row_t[...])
-    for k in range(4):
-        gpart[k, 0] = gram[24 * k : 24 * k + 24]
+    for i, ref in enumerate((row_t, bandx_t)):
+        gram = exact(ref[...].T, ref[...])
+        for k in range(4):
+            gpart[k, i] = gram[24 * k : 24 * k + 24]
+    grecv[a] = gpart[p]
+    for to in gx_peers:
+        send(gpart.at[p], grecv.at[a], S_GRAM, (to, g))
+    arrived(colg.at[0, pl.ds(0, NLZ - 1)], S_COL)
+    send(colg.at[c], colg.at[c], S_COLC, (a, partner))
 
     @pl.loop(0, CHUNKS)
     def _(n):
         send_pieces(n)
-
-    arrived(colg.at[0, pl.ds(0, NLZ - 1)], S_COL)
-    send(colg.at[c], colg.at[c], S_COLC, (a, partner))
-    arrived(bandx.at[pl.ds(0, NY - 1)], S_BANDX)
-    for k in range(NY):
-        bandx_t[BW * k : BW * k + BW] = bandx[k]
-    gram = exact(bandx_t[...].T, bandx_t[...])
-    for k in range(4):
-        gpart[k, 1] = gram[24 * k : 24 * k + 24]
-    grecv[a] = gpart[p]
-    for to in gx_peers:
-        send(gpart.at[p], grecv.at[a], S_GRAM, (to, g))
 
     arrived(colg.at[0], S_COLC)
     for i in range(2):
@@ -258,13 +250,26 @@
             colf[at : at + CW] = block
             low[at : at + CW] = block.astype(BF16)
 
+    fpart[...] = jnp.zeros_like(fpart)
     for t in range(FRAMES):
         fpart[t : t + 1] = jnp.sum(
             by_frame[t] * low[...].astype(F32), axis=0, keepdims=True
         )
-    fg[g] = fpart[...]
-    for to in gy_peers:
-        send(fpart, fg.at[g], S_F1, (a, to))
+
+    def send_rows(q):
+        span = pl.ds(q * PER, PER)
+        arrived(rcore.at[span], S_T1 + q)
+        rsum[span] = rsend[c, span] + rcore[span]
+        for i in range(PER):
+            k = slot_lz(q, i)
+
+            @pl.when(k != lz)
+            def _():
+                send(rsum.at[q * PER + i], rrecv.at[lz], S_ROWS, (a, k * 2 + c))
+
+            @pl.when(k == lz)
+            def _():
+                rrecv[lz] = rsum[q * PER + i]
 
     @pl.loop(0, 4)
     def _(q):
@@ -279,40 +284,39 @@
             rows = rows + block * tb_t[j : j + 1]
             block = block * row_here
             partials[q, j] = jnp.sum(block.reshape(QROWS // 8, 8, LANES), axis=0)
-        owners = [(i // 4) * (NY // 2) + 4 * q + i % 4 for i in range(NY // 4)]
-        for i, k in enumerate(owners):
-            rsend[k] = rows[RW * i : RW * i + RW]
-        for k in owners:
-
-            @pl.when(k != g)
-            def _():
-                send(rsend.at[k], rrecv.at[g], S_ROWS, (a, k))
+        frames = fpart[...]
+        for i in range(NY // 4):
+            rsend[i % 2, q * PER + i // 2, 0:RW] = rows[RW * i : RW * i + RW]
+            rsend[i % 2, q * PER + i // 2, RW : 2 * RW] = frames
+        span = pl.ds(q * PER, PER)
+        send(rsend.at[other, span], rcore.at[span], S_T1 + q, (a, partner))
+
+    @pl.loop(0, 4)
+    def _(q):
+        send_rows(q)
 
     sums = total(partials, 4)
     bands = jnp.zeros((BANDS, LANES), F32)
     for t in range(FRAMES):
         bands = bands + time8[t : t + 1] * jnp.sum(sums[t * BANDS : (t + 1) * BANDS], axis=1)
+
+    arrived(recv2.at[pl.ds(0, NLZ - 1)], S_R2)
+    fin = total(recv2, NLZ)
     for k in range(NX):
-        bsend[k] = bands[BW * k : BW * k + BW]
-    for k in range(1, NX):
-        to = wrap(a + k, NX)
-        send(bsend.at[to], brecv.at[a], S_BANDS, (to, g))
-    brecv[a] = bsend[a]
-    rrecv[g] = rsend[g]
-
+        xsend[k, 0:PACK] = fin
+        xsend[k, PACK : PACK + BW] = bands[BW * k : BW * k + BW]
+    recv3[a] = xsend[a]
+    for to in gx_peers:
+        send(xsend.at[to], recv3.at[a], S_R3, (to, g))
     arrived(grecv.at[pl.ds(0, NX - 1)], S_GRAM)
     gall[p] = total(grecv, NX)
     for k in range(1, 4):
         to = wrap(p + k, 4)
         to_l = lax.div(to, 2)
         send(gall.at[p], gall.at[p], S_GRAMP, (a, (to_l * 8 + z) * 2 + to - 2 * to_l))
-    arrived(recv2.at[pl.ds(0, NLZ - 1)], S_R2)
-    fin[...] = total(recv2, NLZ)
-    recv3[a] = fin[...]
-    for to in gx_peers:
-        send(fin, recv3.at[a], S_R3, (to, g))
-    arrived(fg.at[pl.ds(0, NY - 1)], S_F1)
-    fsum[...] = total(fg, NY)
+    arrived(rrecv.at[pl.ds(0, NLZ - 1)], S_ROWS)
+    row_sums = total(rrecv, NLZ)
+    fsum[...] = row_sums[RW : RW + FRAMES]
     fx[a] = fsum[...]
     for to in gx_peers:
         send(fsum, fx.at[a], S_F2, (to, g))
@@ -337,32 +341,30 @@
     band_model = exact(packed[CW:MSG], gram_rows * gram_cols * gram_time)
     time_model = exact(time8, gram_rows * gram_cols * gram_bands)
 
+    row_out[...] = (row_model[0:RW] - row_sums[0:RW])[:, 0:RANK]
+    arrived(recv3.at[pl.ds(0, NX - 1)], S_R3)
+    sums = total(recv3, NX)
+    band_out[...] = (band_model[0:BW] - sums[PACK : PACK + BW])[:, 0:RANK]
+    sums = jnp.concatenate(unpack([sums[8 * m : 8 * m + 8] for m in range(3)]), axis=0)
+    col_out[...] = (col_model - sums)[:, 0:RANK]
     arrived(fx.at[pl.ds(0, NX - 1)], S_F2)
     time_out[...] = (time_model[0:FRAMES] - total(fx, NX))[:, 0:RANK]
-    arrived(recv3.at[pl.ds(0, NX - 1)], S_R3)
-    sums = total(recv3, NX)
-    sums = jnp.concatenate(unpack([sums[8 * m : 8 * m + 8] for m in range(3)]), axis=0)
-    col_out[...] = (col_model - sums)[:, 0:RANK]
-    arrived(rrecv.at[pl.ds(0, NY - 1)], S_ROWS)
-    row_out[...] = (row_model[0:RW] - total(rrecv, NY))[:, 0:RANK]
-    arrived(brecv.at[pl.ds(0, NX - 1)], S_BANDS)
-    band_out[...] = (band_model[0:BW] - total(brecv, NX))[:, 0:RANK]
-
-    sent(rowg.at[pl.ds(0, NY - 1)], S_ROW)
+
+    sent(rowg.at[0, pl.ds(0, NLZ - 1)], S_ROW)
+    sent(rowg.at[0], S_ROWC)
     sent(bandg.at[pl.ds(0, NX - 1)], S_BAND)
-    sent(bandx.at[pl.ds(0, NY - 1)], S_BANDX)
     sent(colg.at[0, pl.ds(0, NLZ - 1)], S_COL)
     sent(colg.at[0], S_COLC)
     for n in range(CHUNKS):
         sent(recv1.at[pl.ds(n * PER, PER)], S_R1 + n)
     sent(recv2.at[pl.ds(0, NLZ - 1)], S_R2)
     sent(recv3.at[pl.ds(0, NX - 1)], S_R3)
-    sent(fg.at[pl.ds(0, NY - 1)], S_F1)
     sent(fx.at[pl.ds(0, NX - 1)], S_F2)
     sent(grecv.at[pl.ds(0, NX - 1)], S_GRAM)
     sent(gall.at[pl.ds(0, 3)], S_GRAMP)
-    sent(rrecv.at[pl.ds(0, NY - 1)], S_ROWS)
-    sent(brecv.at[pl.ds(0, NX - 1)], S_BANDS)
+    for q in range(4):
+        sent(rcore.at[pl.ds(q * PER, PER)], S_T1 + q)
+    sent(rrecv.at[pl.ds(0, NLZ - 1)], S_ROWS)
 
 
 def hand_over(*refs):
@@ -393,14 +395,12 @@
             v((BW, RANK), F32),
             v((FRAMES, RANK), F32),
             v((TB, ROWS, COLS), BF16),
-            v((RW, LANES), F32),
             v((BW, LANES), F32),
-            v((NY, RW, LANES), F32),
+            v((2, NLZ, 8, LANES), F32),
             v((NX, BW, LANES), F32),
-            v((NY, BW, LANES), F32),
             v((ROWS, LANES), F32),
             v((BANDS, LANES), F32),
-            v((NY * BW, LANES), F32),
+            v((NY * RW, LANES), F32),
             v((LANES, LANES), F32),
             v((COLS, TB * ROWS), BF16),
             v((FRAMES, HALF, 2 * LANES), BF16),
@@ -409,25 +409,24 @@
             v((NLZ, PACK, LANES), F32),
             v((NLZ, PACK, LANES), F32),
             v((NLZ, PACK, LANES), F32),
-            v((PACK, LANES), F32),
-            v((NX, PACK, LANES), F32),
+            v((NX, PACK + 8, LANES), F32),
+            v((NX, PACK + 8, LANES), F32),
             v((2, NLZ, PACK, LANES), F32),
             v((COLS, LANES), F32),
             v((COLS, LANES), BF16),
             v((TB * QROWS, LANES), F32),
             v((4, TB, 8, LANES), F32),
-            v((FRAMES, LANES), F32),
-            v((NY, FRAMES, LANES), F32),
+            v((RW, LANES), F32),
             v((FRAMES, LANES), F32),
             v((NX, FRAMES, LANES), F32),
             v((4, 2, 24, LANES), F32),
             v((NX, 2, 24, LANES), F32),
             v((4, 2, 24, LANES), F32),
             v((LANES, LANES), F32),
-            v((NY, RW, LANES), F32),
-            v((NY, RW, LANES), F32),
-            v((NX, BW, LANES), F32),
-            v((NX, BW, LANES), F32),
+            v((2, NLZ, 8, LANES), F32),
+            v((NLZ, 8, LANES), F32),
+            v((NLZ, 8, LANES), F32),
+            v((NLZ, 8, LANES), F32),
             pltpu.SemaphoreType.DMA((LOADS + 4,)),
             pltpu.SemaphoreType.DMA((N_SEMS,)),
             pltpu.SemaphoreType.DMA((N_SEMS,)),

time: 36.5 us -> 37.4 us (1.025)
  Pallas kernels: 35.8 us -> 36.7 us
    pallas_call x1, Pallas kernels: 35.1 us -> 36 us  [shards(): pl.pallas_call(kernel, out_shape=shapes, in_specs=[pl.BlockSpec(memory_sp...]
where the time goes in v6:
time: 37.4 us; the launch traced here: 37.3 us
  Pallas kernels  36.7 us (98%)
  between operations  0.64 us (2%)
    pallas_call x1, Pallas kernels, shards(): pl.pallas_call(kernel, out_shape=shapes, in_specs=[pl.BlockSpec(memory_sp...  36 us

profile of v6, /device:TPU:1, one launch (start us, length us, event | category | flops | bytes accessed | tf_op | source)
XLA Modules:
  0.0 37.3 jit_solution(18419071324389748889)
XLA Ops:
  0.6 36.0 %shard_map.84 = (f32[4,96]{1,0:T(4,128)S(1)}, f32[32,96]{1,0:T(8,128)S(1)}, f32[2,96]{1,0:T(2,128)S(1)}, f32[2,96]{1,0:T(2,128)S(1)}) custom-call(bf16[32,128,1024]{2,1,0:T(8,128)(2,1)} %bitcast.9, f32[4,96]{1,0:T(4,128)} %bitcast.11, f32[32,96]{1,0:T(8,128)} %bitcast.10, f32[2,96]{1,0:T(2,128)} %bitcast.12, f32[2,96]{1,0:T(2,128)} %bitcast.13), custom_call_target="tpu_custom_call" | custom-call | flops 1610612736 | bytes 8388608 | tf_op jit(solution)/shard_map/pallas_call | solution.py:386
  36.7 0.7 %shard_map.85 = (f32[4,96]{1,0:T(4,128)}, f32[32,96]{1,0:T(8,128)}, f32[2,96]{1,0:T(2,128)}, f32[2,96]{1,0:T(2,128)}) custom-call(f32[4,96]{1,0:T(4,128)S(1)} %get-tuple-element.12.refs_0_, f32[32,96]{1,0:T(8,128)S(1)} %get-tuple-element.13.refs_1_, f32[2,96]{1,0:T(2,128)S(1)} %get-tuple-element.14.refs_2_, f32[2,96]{1,0:T(2,128)S(1)} %get-tuple-element.15.refs_3_), custom_call_target="tpu_custom_call" | custom-call | tf_op jit(solution)/shard_map/pallas_call | solution.py:444

commit v7 on v5

--- a/solution.py
+++ b/solution.py
@@ -152,6 +152,8 @@
         send(mine2, bandg.at[a], S_BAND, (to, g))
     for to in core_peers:
         send(colg.at[c, lz], colg.at[c, lz], S_COL, (a, to))
+    for to in gy_peers:
+        send(mine2, bandx.at[g], S_BANDX, (a, to))
 
     @pl.loop(0, LOADS)
     def _(k):
@@ -162,8 +164,6 @@
             at = pl.multiple_of((k * per + i) * ROWS, ROWS)
             turned[:, pl.ds(at, ROWS)] = data[k * per + i].T
 
-    for to in gy_peers:
-        send(mine2, bandx.at[g], S_BANDX, (a, to))
 
     arrived(bandg.at[pl.ds(0, NX - 1)], S_BAND)
     for k in range(NX):
@@ -225,27 +225,42 @@
             for m in range(3):
                 part[k % 2, n * PER + k // 2, 8 * m : 8 * m + 8] = tiles[m][8 * k : 8 * k + 8]
         span = pl.ds(n * PER, PER)
-        send(part.at[other, span], recv1.at[span], S_R1 + n, (a, partner))
-
-    gram = exact(row_t[...].T, row_t[...])
-    for k in range(4):
-        gpart[k, 0] = gram[24 * k : 24 * k + 24]
-
-    @pl.loop(0, CHUNKS)
-    def _(n):
-        send_pieces(n)
+
+        @pl.when(n == 0)
+        def _():
+            for i in range(PER):
+                for j in range(2):
+                    to = slot_lz(0, i) * 2 + j
+
+                    @pl.when(to != g)
+                    def _():
+                        send(part.at[j, i], recv2.at[c * NLZ + lz], S_R2, (a, to))
+
+                    @pl.when(to == g)
+                    def _():
+                        recv2[c * NLZ + lz] = part[j, i]
+
+        @pl.when(n > 0)
+        def _():
+            send(part.at[other, span], recv1.at[span], S_R1 + n, (a, partner))
 
     arrived(colg.at[0, pl.ds(0, NLZ - 1)], S_COL)
     send(colg.at[c], colg.at[c], S_COLC, (a, partner))
+
     arrived(bandx.at[pl.ds(0, NY - 1)], S_BANDX)
     for k in range(NY):
         bandx_t[BW * k : BW * k + BW] = bandx[k]
-    gram = exact(bandx_t[...].T, bandx_t[...])
-    for k in range(4):
-        gpart[k, 1] = gram[24 * k : 24 * k + 24]
+    for i, ref in enumerate((row_t, bandx_t)):
+        gram = exact(ref[...].T, ref[...])
+        for k in range(4):
+            gpart[k, i] = gram[24 * k : 24 * k + 24]
     grecv[a] = gpart[p]
     for to in gx_peers:
         send(gpart.at[p], grecv.at[a], S_GRAM, (to, g))
+
+    @pl.loop(1, CHUNKS)
+    def _(n):
+        send_pieces(n)
 
     arrived(colg.at[0], S_COLC)
     for i in range(2):
@@ -306,8 +321,17 @@
         to = wrap(p + k, 4)
         to_l = lax.div(to, 2)
         send(gall.at[p], gall.at[p], S_GRAMP, (a, (to_l * 8 + z) * 2 + to - 2 * to_l))
-    arrived(recv2.at[pl.ds(0, NLZ - 1)], S_R2)
-    fin[...] = total(recv2, NLZ)
+
+    @pl.when(z < 2)
+    def _():
+        arrived(recv2.at[pl.ds(0, NY - 1)], S_R2)
+        fin[...] = total(recv2, NY)
+
+    @pl.when(z >= 2)
+    def _():
+        arrived(recv2.at[pl.ds(0, NLZ - 1)], S_R2)
+        fin[...] = total(recv2, NLZ)
+
     recv3[a] = fin[...]
     for to in gx_peers:
         send(fin, recv3.at[a], S_R3, (to, g))
@@ -353,9 +377,9 @@
     sent(bandx.at[pl.ds(0, NY - 1)], S_BANDX)
     sent(colg.at[0, pl.ds(0, NLZ - 1)], S_COL)
     sent(colg.at[0], S_COLC)
-    for n in range(CHUNKS):
+    for n in range(1, CHUNKS):
         sent(recv1.at[pl.ds(n * PER, PER)], S_R1 + n)
-    sent(recv2.at[pl.ds(0, NLZ - 1)], S_R2)
+    sent(recv2.at[pl.ds(0, 2 * PER + (CHUNKS - 1) * PER - 1)], S_R2)
     sent(recv3.at[pl.ds(0, NX - 1)], S_R3)
     sent(fg.at[pl.ds(0, NY - 1)], S_F1)
     sent(fx.at[pl.ds(0, NX - 1)], S_F2)
@@ -408,7 +432,7 @@
             v((2, NLZ, PACK, LANES), F32),
             v((NLZ, PACK, LANES), F32),
             v((NLZ, PACK, LANES), F32),
-            v((NLZ, PACK, LANES), F32),
+            v((NY, PACK, LANES), F32),
             v((PACK, LANES), F32),
             v((NX, PACK, LANES), F32),
             v((2, NLZ, PACK, LANES), F32),

time: 36.5 us -> 36.8 us (level)
  no operation moved by 1% of the time
where the time goes in v7:
time: 36.8 us; the launch traced here: 36.7 us
  Pallas kernels  36 us (98%)
  between operations  0.64 us (2%)
    pallas_call x1, Pallas kernels, shards(): pl.pallas_call(kernel, out_shape=shapes, in_specs=[pl.BlockSpec(memory_sp...  35.4 us

profile of v7, /device:TPU:1, one launch (start us, length us, event | category | flops | bytes accessed | tf_op | source)
XLA Modules:
  0.0 36.7 jit_solution(16408681993159180252)
XLA Ops:
  0.6 35.4 %shard_map.84 = (f32[4,96]{1,0:T(4,128)S(1)}, f32[32,96]{1,0:T(8,128)S(1)}, f32[2,96]{1,0:T(2,128)S(1)}, f32[2,96]{1,0:T(2,128)S(1)}) custom-call(bf16[32,128,1024]{2,1,0:T(8,128)(2,1)} %bitcast.9, f32[4,96]{1,0:T(4,128)} %bitcast.11, f32[32,96]{1,0:T(8,128)} %bitcast.10, f32[2,96]{1,0:T(2,128)} %bitcast.12, f32[2,96]{1,0:T(2,128)} %bitcast.13), custom_call_target="tpu_custom_call" | custom-call | flops 1610612736 | bytes 8388608 | tf_op jit(solution)/shard_map/pallas_call | solution.py:408
  36.0 0.7 %shard_map.85 = (f32[4,96]{1,0:T(4,128)}, f32[32,96]{1,0:T(8,128)}, f32[2,96]{1,0:T(2,128)}, f32[2,96]{1,0:T(2,128)}) custom-call(f32[4,96]{1,0:T(4,128)S(1)} %get-tuple-element.12.refs_0_, f32[32,96]{1,0:T(8,128)S(1)} %get-tuple-element.13.refs_1_, f32[2,96]{1,0:T(2,128)S(1)} %get-tuple-element.14.refs_2_, f32[2,96]{1,0:T(2,128)S(1)} %get-tuple-element.15.refs_3_), custom_call_target="tpu_custom_call" | custom-call | tf_op jit(solution)/shard_map/pallas_call | solution.py:469

commit v8 on v5

--- a/solution.py
+++ b/solution.py
@@ -144,6 +144,16 @@
     for m, tile in enumerate(pack([packed[8 * m : 8 * m + 8] for m in range(4)])):
         colg[c, lz, 8 * m : 8 * m + 8] = tile
 
+    def turn(k):
+        per = TB // LOADS
+        span = pl.ds(k * per, per)
+        pltpu.make_async_copy(tensor.at[span], data.at[span], local_sems.at[k]).wait()
+        for i in range(per):
+            at = pl.multiple_of((k * per + i) * ROWS, ROWS)
+            turned[:, pl.ds(at, ROWS)] = data[k * per + i].T
+
+    early = jnp.where(z == 0, 6, jnp.where(z == 1, 5, jnp.where(z == 2, 3, jnp.where(z == 3, 1, 0))))
+    pl.loop(0, early)(turn)
     pl.semaphore_wait(barrier, NY - 1 + NX - 1)
 
     for to in gy_peers:
@@ -153,14 +163,7 @@
     for to in core_peers:
         send(colg.at[c, lz], colg.at[c, lz], S_COL, (a, to))
 
-    @pl.loop(0, LOADS)
-    def _(k):
-        per = TB // LOADS
-        span = pl.ds(k * per, per)
-        pltpu.make_async_copy(tensor.at[span], data.at[span], local_sems.at[k]).wait()
-        for i in range(per):
-            at = pl.multiple_of((k * per + i) * ROWS, ROWS)
-            turned[:, pl.ds(at, ROWS)] = data[k * per + i].T
+    pl.loop(early, LOADS)(turn)
 
     for to in gy_peers:
         send(mine2, bandx.at[g], S_BANDX, (a, to))

time: 36.5 us -> 36.5 us (level)
  no operation moved by 1% of the time
where the time goes in v8:
time: 36.5 us; the launch traced here: 36.4 us
  Pallas kernels  35.8 us (98%)
  between operations  0.64 us (2%)
    pallas_call x1, Pallas kernels, shards(): pl.pallas_call(kernel, out_shape=shapes, in_specs=[pl.BlockSpec(memory_sp...  35.1 us

profile of v8, /device:TPU:1, one launch (start us, length us, event | category | flops | bytes accessed | tf_op | source)
XLA Modules:
  0.0 36.4 jit_solution(15910730098966132236)
XLA Ops:
  0.6 35.1 %shard_map.84 = (f32[4,96]{1,0:T(4,128)S(1)}, f32[32,96]{1,0:T(8,128)S(1)}, f32[2,96]{1,0:T(2,128)S(1)}, f32[2,96]{1,0:T(2,128)S(1)}) custom-call(bf16[32,128,1024]{2,1,0:T(8,128)(2,1)} %bitcast.9, f32[4,96]{1,0:T(4,128)} %bitcast.11, f32[32,96]{1,0:T(8,128)} %bitcast.10, f32[2,96]{1,0:T(2,128)} %bitcast.12, f32[2,96]{1,0:T(2,128)} %bitcast.13), custom_call_target="tpu_custom_call" | custom-call | flops 1610612736 | bytes 8388608 | tf_op jit(solution)/shard_map/pallas_call | solution.py:387
  35.8 0.7 %shard_map.85 = (f32[4,96]{1,0:T(4,128)}, f32[32,96]{1,0:T(8,128)}, f32[2,96]{1,0:T(2,128)}, f32[2,96]{1,0:T(2,128)}) custom-call(f32[4,96]{1,0:T(4,128)S(1)} %get-tuple-element.12.refs_0_, f32[32,96]{1,0:T(8,128)S(1)} %get-tuple-element.13.refs_1_, f32[2,96]{1,0:T(2,128)S(1)} %get-tuple-element.14.refs_2_, f32[2,96]{1,0:T(2,128)S(1)} %get-tuple-element.15.refs_3_), custom_call_target="tpu_custom_call" | custom-call | tf_op jit(solution)/shard_map/pallas_call | solution.py:448

commit v9 on v5

--- a/solution.py
+++ b/solution.py
@@ -92,9 +92,14 @@
     p = l * 2 + c
     other = 1 - c
     partner = lz * 2 + other
-    gy_peers = [wrap(g + k, NY) for k in range(1, NY)]
-    gx_peers = [wrap(a + k, NX) for k in range(1, NX)]
-    core_peers = [wrap(lz + k, NLZ) * 2 + c for k in range(1, NLZ)]
+    def gy_peers(act):
+        pl.loop(1, NY)(lambda k: act((a, wrap(g + k, NY))))
+
+    def gx_peers(act):
+        pl.loop(1, NX)(lambda k: act((wrap(a + k, NX), g)))
+
+    def core_peers(act):
+        pl.loop(1, NLZ)(lambda k: act((a, wrap(lz + k, NLZ) * 2 + c)))
 
     def send(src, dst, sem, device):
         pltpu.make_async_remote_copy(
@@ -118,10 +123,11 @@
         copy.start()
 
     barrier = pltpu.get_barrier_semaphore()
-    for to in gy_peers:
-        pl.semaphore_signal(barrier, inc=1, device_id=(a, to), device_id_type=MESH)
-    for to in gx_peers:
-        pl.semaphore_signal(barrier, inc=1, device_id=(to, g), device_id_type=MESH)
+    def greet(to):
+        pl.semaphore_signal(barrier, inc=1, device_id=to, device_id_type=MESH)
+
+    gy_peers(greet)
+    gx_peers(greet)
 
     for k in range(LOADS):
         span = pl.ds(k * (TB // LOADS), TB // LOADS)
@@ -146,12 +152,9 @@
 
     pl.semaphore_wait(barrier, NY - 1 + NX - 1)
 
-    for to in gy_peers:
-        send(mine4, rowg.at[g], S_ROW, (a, to))
-    for to in gx_peers:
-        send(mine2, bandg.at[a], S_BAND, (to, g))
-    for to in core_peers:
-        send(colg.at[c, lz], colg.at[c, lz], S_COL, (a, to))
+    gy_peers(lambda to: send(mine4, rowg.at[g], S_ROW, to))
+    gx_peers(lambda to: send(mine2, bandg.at[a], S_BAND, to))
+    core_peers(lambda to: send(colg.at[c, lz], colg.at[c, lz], S_COL, to))
 
     @pl.loop(0, LOADS)
     def _(k):
@@ -162,8 +165,7 @@
             at = pl.multiple_of((k * per + i) * ROWS, ROWS)
             turned[:, pl.ds(at, ROWS)] = data[k * per + i].T
 
-    for to in gy_peers:
-        send(mine2, bandx.at[g], S_BANDX, (a, to))
+    gy_peers(lambda to: send(mine2, bandx.at[g], S_BANDX, to))
 
     arrived(bandg.at[pl.ds(0, NX - 1)], S_BAND)
     for k in range(NX):
@@ -184,23 +186,20 @@
             prod[t, span, 0:LANES] = (tb_t[pl.ds(t * BANDS + k, 1)] * rows).astype(BF16)
             prod[t, span, LANES:] = plain
 
-    def slot_lz(n, i):
-        return (i // 2) * (NLZ // 2) + 2 * n + i % 2
-
     def send_pieces(n):
-        span = pl.ds(n * PER, PER)
-        arrived(recv1.at[span], S_R1 + n)
-        sum1[span] = part[c, span] + recv1[span]
-        for i in range(PER):
-            k = slot_lz(n, i)
-
-            @pl.when(k != lz)
+        arrived(recv1.at[pl.ds(0, 3), pl.ds(0, 2)], S_R1 + n)
+        for i in range(2):
+            k = 2 * n + i
+            recv1[p, k] = part[p, k]
+            sum1[k] = recv1[0, k] + recv1[1, k] + recv1[2, k] + recv1[3, k]
+
+            @pl.when(k != z)
             def _():
-                send(sum1.at[n * PER + i], recv2.at[lz], S_R2, (a, k * 2 + c))
-
-            @pl.when(k == lz)
+                send(sum1.at[k], recv2.at[z], S_R2, (a, (l * 8 + k) * 2 + c))
+
+            @pl.when(k == z)
             def _():
-                recv2[lz] = sum1[n * PER + i]
+                recv2[z] = sum1[k]
 
     @pl.loop(0, CHUNKS)
     def _(n):
@@ -223,9 +222,16 @@
         tiles = pack([acc[:, m].reshape(CHUNK // 4, LANES) for m in range(4)])
         for k in range(CHUNK // CW):
             for m in range(3):
-                part[k % 2, n * PER + k // 2, 8 * m : 8 * m + 8] = tiles[m][8 * k : 8 * k + 8]
-        span = pl.ds(n * PER, PER)
-        send(part.at[other, span], recv1.at[span], S_R1 + n, (a, partner))
+                at = (k // 4) * 2 + k % 2, 2 * n + (k // 2) % 2
+                part[at[0], at[1], 8 * m : 8 * m + 8] = tiles[m][8 * k : 8 * k + 8]
+        span = pl.ds(2 * n, 2)
+        for k in range(1, 4):
+            to = wrap(p + k, 4)
+            to_l = lax.div(to, 2)
+            send(
+                part.at[to, span], recv1.at[p, span], S_R1 + n,
+                (a, (to_l * 8 + z) * 2 + to - 2 * to_l),
+            )
 
     gram = exact(row_t[...].T, row_t[...])
     for k in range(4):
@@ -244,8 +250,7 @@
     for k in range(4):
         gpart[k, 1] = gram[24 * k : 24 * k + 24]
     grecv[a] = gpart[p]
-    for to in gx_peers:
-        send(gpart.at[p], grecv.at[a], S_GRAM, (to, g))
+    gx_peers(lambda to: send(gpart.at[p], grecv.at[a], S_GRAM, to))
 
     arrived(colg.at[0], S_COLC)
     for i in range(2):
@@ -263,8 +268,7 @@
             by_frame[t] * low[...].astype(F32), axis=0, keepdims=True
         )
     fg[g] = fpart[...]
-    for to in gy_peers:
-        send(fpart, fg.at[g], S_F1, (a, to))
+    gy_peers(lambda to: send(fpart, fg.at[g], S_F1, to))
 
     @pl.loop(0, 4)
     def _(q):
@@ -294,9 +298,7 @@
         bands = bands + time8[t : t + 1] * jnp.sum(sums[t * BANDS : (t + 1) * BANDS], axis=1)
     for k in range(NX):
         bsend[k] = bands[BW * k : BW * k + BW]
-    for k in range(1, NX):
-        to = wrap(a + k, NX)
-        send(bsend.at[to], brecv.at[a], S_BANDS, (to, g))
+    gx_peers(lambda to: send(bsend.at[to[0]], brecv.at[a], S_BANDS, to))
     brecv[a] = bsend[a]
     rrecv[g] = rsend[g]
 
@@ -306,16 +308,14 @@
         to = wrap(p + k, 4)
         to_l = lax.div(to, 2)
         send(gall.at[p], gall.at[p], S_GRAMP, (a, (to_l * 8 + z) * 2 + to - 2 * to_l))
-    arrived(recv2.at[pl.ds(0, NLZ - 1)], S_R2)
-    fin[...] = total(recv2, NLZ)
+    arrived(recv2.at[pl.ds(0, 7)], S_R2)
+    fin[...] = total(recv2, 8)
     recv3[a] = fin[...]
-    for to in gx_peers:
-        send(fin, recv3.at[a], S_R3, (to, g))
+    gx_peers(lambda to: send(fin, recv3.at[a], S_R3, to))
     arrived(fg.at[pl.ds(0, NY - 1)], S_F1)
     fsum[...] = total(fg, NY)
     fx[a] = fsum[...]
-    for to in gx_peers:
-        send(fsum, fx.at[a], S_F2, (to, g))
+    gx_peers(lambda to: send(fsum, fx.at[a], S_F2, to))
 
     gcols[...] = jnp.zeros_like(gcols)
 
@@ -354,8 +354,8 @@
     sent(colg.at[0, pl.ds(0, NLZ - 1)], S_COL)
     sent(colg.at[0], S_COLC)
     for n in range(CHUNKS):
-        sent(recv1.at[pl.ds(n * PER, PER)], S_R1 + n)
-    sent(recv2.at[pl.ds(0, NLZ - 1)], S_R2)
+        sent(recv1.at[pl.ds(0, 3), pl.ds(0, 2)], S_R1 + n)
+    sent(recv2.at[pl.ds(0, 7)], S_R2)
     sent(recv3.at[pl.ds(0, NX - 1)], S_R3)
     sent(fg.at[pl.ds(0, NY - 1)], S_F1)
     sent(fx.at[pl.ds(0, NX - 1)], S_F2)
@@ -405,10 +405,10 @@
             v((COLS, TB * ROWS), BF16),
             v((FRAMES, HALF, 2 * LANES), BF16),
             v((FRAMES, COLS, LANES), F32),
-            v((2, NLZ, PACK, LANES), F32),
-            v((NLZ, PACK, LANES), F32),
-            v((NLZ, PACK, LANES), F32),
-            v((NLZ, PACK, LANES), F32),
+            v((4, 8, PACK, LANES), F32),
+            v((4, 8, PACK, LANES), F32),
+            v((8, PACK, LANES), F32),
+            v((8, PACK, LANES), F32),
             v((PACK, LANES), F32),
             v((NX, PACK, LANES), F32),
             v((2, NLZ, PACK, LANES), F32),

time: 36.5 us -> 37.6 us (1.030)
  Pallas kernels: 35.8 us -> 36.8 us
    pallas_call x1, Pallas kernels: 35.1 us -> 36.1 us  [shards(): pl.pallas_call(kernel, out_shape=shapes, in_specs=[pl.BlockSpec(memory_sp...]
where the time goes in v9:
time: 37.6 us; the launch traced here: 37.4 us
  Pallas kernels  36.8 us (98%)
  between operations  0.64 us (2%)
    pallas_call x1, Pallas kernels, shards(): pl.pallas_call(kernel, out_shape=shapes, in_specs=[pl.BlockSpec(memory_sp...  36.1 us

profile of v9, /device:TPU:1, one launch (start us, length us, event | category | flops | bytes accessed | tf_op | source)
XLA Modules:
  0.0 37.4 jit_solution(5329302464198532062)
XLA Ops:
  0.6 36.1 %shard_map.84 = (f32[4,96]{1,0:T(4,128)S(1)}, f32[32,96]{1,0:T(8,128)S(1)}, f32[2,96]{1,0:T(2,128)S(1)}, f32[2,96]{1,0:T(2,128)S(1)}) custom-call(bf16[32,128,1024]{2,1,0:T(8,128)(2,1)} %bitcast.9, f32[4,96]{1,0:T(4,128)} %bitcast.11, f32[32,96]{1,0:T(8,128)} %bitcast.10, f32[2,96]{1,0:T(2,128)} %bitcast.12, f32[2,96]{1,0:T(2,128)} %bitcast.13), custom_call_target="tpu_custom_call" | custom-call | flops 1610612736 | bytes 8388608 | tf_op jit(solution)/shard_map/pallas_call | solution.py:384
  36.8 0.7 %shard_map.85 = (f32[4,96]{1,0:T(4,128)}, f32[32,96]{1,0:T(8,128)}, f32[2,96]{1,0:T(2,128)}, f32[2,96]{1,0:T(2,128)}) custom-call(f32[4,96]{1,0:T(4,128)S(1)} %get-tuple-element.12.refs_0_, f32[32,96]{1,0:T(8,128)S(1)} %get-tuple-element.13.refs_1_, f32[2,96]{1,0:T(2,128)S(1)} %get-tuple-element.14.refs_2_, f32[2,96]{1,0:T(2,128)S(1)} %get-tuple-element.15.refs_3_), custom_call_target="tpu_custom_call" | custom-call | tf_op jit(solution)/shard_map/pallas_call | solution.py:445

commit v10 on v5

--- a/solution.py
+++ b/solution.py
@@ -6,7 +6,6 @@
 from jax.sharding import PartitionSpec as P
 
 MESH = pl.DeviceIdType.MESH
-HIGHEST = lax.Precision.HIGHEST
 F32 = jnp.float32
 BF16 = jnp.bfloat16
 
@@ -36,7 +35,10 @@
 
 
 def exact(x, y):
-    return jnp.dot(x, y, precision=HIGHEST, preferred_element_type=F32)
+    x_high, y_high = x.astype(BF16), y.astype(BF16)
+    x_low = (x - x_high.astype(F32)).astype(BF16)
+    y_low = (y - y_high.astype(F32)).astype(BF16)
+    return dot(x_high, y_high) + (dot(x_high, y_low) + dot(x_low, y_high))
 
 
 def total(ref, count):
@@ -230,13 +232,13 @@
     gram = exact(row_t[...].T, row_t[...])
     for k in range(4):
         gpart[k, 0] = gram[24 * k : 24 * k + 24]
+    arrived(colg.at[0, pl.ds(0, NLZ - 1)], S_COL)
+    send(colg.at[c], colg.at[c], S_COLC, (a, partner))
 
     @pl.loop(0, CHUNKS)
     def _(n):
         send_pieces(n)
 
-    arrived(colg.at[0, pl.ds(0, NLZ - 1)], S_COL)
-    send(colg.at[c], colg.at[c], S_COLC, (a, partner))
     arrived(bandx.at[pl.ds(0, NY - 1)], S_BANDX)
     for k in range(NY):
         bandx_t[BW * k : BW * k + BW] = bandx[k]
@@ -306,6 +308,13 @@
         to = wrap(p + k, 4)
         to_l = lax.div(to, 2)
         send(gall.at[p], gall.at[p], S_GRAMP, (a, (to_l * 8 + z) * 2 + to - 2 * to_l))
+    gcols[...] = jnp.zeros_like(gcols)
+
+    @pl.loop(0, 4)
+    def _(i):
+        block = colf[pl.ds(pl.multiple_of(i * 256, 256), 256)]
+        gcols[...] += exact(block.T, block)
+
     arrived(recv2.at[pl.ds(0, NLZ - 1)], S_R2)
     fin[...] = total(recv2, NLZ)
     recv3[a] = fin[...]
@@ -316,13 +325,6 @@
     fx[a] = fsum[...]
     for to in gx_peers:
         send(fsum, fx.at[a], S_F2, (to, g))
-
-    gcols[...] = jnp.zeros_like(gcols)
-
-    @pl.loop(0, 4)
-    def _(i):
-        block = colf[pl.ds(pl.multiple_of(i * 256, 256), 256)]
-        gcols[...] += exact(block.T, block)
 
     gram_cols = gcols[...]
     arrived(gall.at[pl.ds(0, 3)], S_GRAMP)

time: 36.5 us -> 36.7 us (level)
  no operation moved by 1% of the time
where the time goes in v10:
time: 36.7 us; the launch traced here: 36.6 us
  Pallas kernels  35.9 us (98%)
  between operations  0.64 us (2%)
    pallas_call x1, Pallas kernels, shards(): pl.pallas_call(kernel, out_shape=shapes, in_specs=[pl.BlockSpec(memory_sp...  35.3 us

profile of v10, /device:TPU:1, one launch (start us, length us, event | category | flops | bytes accessed | tf_op | source)
XLA Modules:
  0.0 36.6 jit_solution(11003401706564352083)
XLA Ops:
  0.6 35.3 %shard_map.84 = (f32[4,96]{1,0:T(4,128)S(1)}, f32[32,96]{1,0:T(8,128)S(1)}, f32[2,96]{1,0:T(2,128)S(1)}, f32[2,96]{1,0:T(2,128)S(1)}) custom-call(bf16[32,128,1024]{2,1,0:T(8,128)(2,1)} %bitcast.9, f32[4,96]{1,0:T(4,128)} %bitcast.11, f32[32,96]{1,0:T(8,128)} %bitcast.10, f32[2,96]{1,0:T(2,128)} %bitcast.12, f32[2,96]{1,0:T(2,128)} %bitcast.13), custom_call_target="tpu_custom_call" | custom-call | flops 1610612736 | bytes 8388608 | tf_op jit(solution)/shard_map/pallas_call | solution.py:386
  35.9 0.7 %shard_map.85 = (f32[4,96]{1,0:T(4,128)}, f32[32,96]{1,0:T(8,128)}, f32[2,96]{1,0:T(2,128)}, f32[2,96]{1,0:T(2,128)}) custom-call(f32[4,96]{1,0:T(4,128)S(1)} %get-tuple-element.12.refs_0_, f32[32,96]{1,0:T(8,128)S(1)} %get-tuple-element.13.refs_1_, f32[2,96]{1,0:T(2,128)S(1)} %get-tuple-element.14.refs_2_, f32[2,96]{1,0:T(2,128)S(1)} %get-tuple-element.15.refs_3_), custom_call_target="tpu_custom_call" | custom-call | tf_op jit(solution)/shard_map/pallas_call | solution.py:447

commit v11 on v10

--- a/solution.py
+++ b/solution.py
@@ -152,8 +152,6 @@
         send(mine4, rowg.at[g], S_ROW, (a, to))
     for to in gx_peers:
         send(mine2, bandg.at[a], S_BAND, (to, g))
-    for to in core_peers:
-        send(colg.at[c, lz], colg.at[c, lz], S_COL, (a, to))
 
     @pl.loop(0, LOADS)
     def _(k):
@@ -164,6 +162,8 @@
             at = pl.multiple_of((k * per + i) * ROWS, ROWS)
             turned[:, pl.ds(at, ROWS)] = data[k * per + i].T
 
+    for to in core_peers:
+        send(colg.at[c, lz], colg.at[c, lz], S_COL, (a, to))
     for to in gy_peers:
         send(mine2, bandx.at[g], S_BANDX, (a, to))
 

time: 36.7 us -> 37.4 us (1.019)
  Pallas kernels: 35.9 us -> 36.7 us
    pallas_call x1, Pallas kernels: 35.3 us -> 36 us  [shards(): pl.pallas_call(kernel, out_shape=shapes, in_specs=[pl.BlockSpec(memory_sp...]
where the time goes in v11:
time: 37.4 us; the launch traced here: 37.3 us
  Pallas kernels  36.7 us (98%)
  between operations  0.64 us (2%)
    pallas_call x1, Pallas kernels, shards(): pl.pallas_call(kernel, out_shape=shapes, in_specs=[pl.BlockSpec(memory_sp...  36 us

profile of v11, /device:TPU:1, one launch (start us, length us, event | category | flops | bytes accessed | tf_op | source)
XLA Modules:
  0.0 37.3 jit_solution(2128160945081259894)
XLA Ops:
  0.6 36.0 %shard_map.84 = (f32[4,96]{1,0:T(4,128)S(1)}, f32[32,96]{1,0:T(8,128)S(1)}, f32[2,96]{1,0:T(2,128)S(1)}, f32[2,96]{1,0:T(2,128)S(1)}) custom-call(bf16[32,128,1024]{2,1,0:T(8,128)(2,1)} %bitcast.9, f32[4,96]{1,0:T(4,128)} %bitcast.11, f32[32,96]{1,0:T(8,128)} %bitcast.10, f32[2,96]{1,0:T(2,128)} %bitcast.12, f32[2,96]{1,0:T(2,128)} %bitcast.13), custom_call_target="tpu_custom_call" | custom-call | flops 1610612736 | bytes 8388608 | tf_op jit(solution)/shard_map/pallas_call | solution.py:386
  36.7 0.7 %shard_map.85 = (f32[4,96]{1,0:T(4,128)}, f32[32,96]{1,0:T(8,128)}, f32[2,96]{1,0:T(2,128)}, f32[2,96]{1,0:T(2,128)}) custom-call(f32[4,96]{1,0:T(4,128)S(1)} %get-tuple-element.12.refs_0_, f32[32,96]{1,0:T(8,128)S(1)} %get-tuple-element.13.refs_1_, f32[2,96]{1,0:T(2,128)S(1)} %get-tuple-element.14.refs_2_, f32[2,96]{1,0:T(2,128)S(1)} %get-tuple-element.15.refs_3_), custom_call_target="tpu_custom_call" | custom-call | tf_op jit(solution)/shard_map/pallas_call | solution.py:447

commit v12 on v10

--- a/solution.py
+++ b/solution.py
@@ -94,9 +94,11 @@
     p = l * 2 + c
     other = 1 - c
     partner = lz * 2 + other
-    gy_peers = [wrap(g + k, NY) for k in range(1, NY)]
     gx_peers = [wrap(a + k, NX) for k in range(1, NX)]
-    core_peers = [wrap(lz + k, NLZ) * 2 + c for k in range(1, NLZ)]
+    lz_order = [lane + wrap(z + k, 8) for k in (4, 3, 5, 2, 6, 1, 7, 0) for lane in (8 * l, 8 - 8 * l)]
+    del lz_order[-2]
+    core_peers = [to * 2 + c for to in lz_order]
+    gy_peers = [to * 2 + core for to in lz_order for core in (c, other)] + [partner]
 
     def send(src, dst, sem, device):
         pltpu.make_async_remote_copy(

time: 36.7 us -> 36.4 us (level)
  no operation moved by 1% of the time
where the time goes in v12:
time: 36.4 us; the launch traced here: 36.3 us
  Pallas kernels  35.6 us (98%)
  between operations  0.64 us (2%)
    pallas_call x1, Pallas kernels, shards(): pl.pallas_call(kernel, out_shape=shapes, in_specs=[pl.BlockSpec(memory_sp...  35 us

profile of v12, /device:TPU:1, one launch (start us, length us, event | category | flops | bytes accessed | tf_op | source)
XLA Modules:
  0.0 36.3 jit_solution(17763972106275676758)
XLA Ops:
  0.6 35.0 %shard_map.84 = (f32[4,96]{1,0:T(4,128)S(1)}, f32[32,96]{1,0:T(8,128)S(1)}, f32[2,96]{1,0:T(2,128)S(1)}, f32[2,96]{1,0:T(2,128)S(1)}) custom-call(bf16[32,128,1024]{2,1,0:T(8,128)(2,1)} %bitcast.9, f32[4,96]{1,0:T(4,128)} %bitcast.11, f32[32,96]{1,0:T(8,128)} %bitcast.10, f32[2,96]{1,0:T(2,128)} %bitcast.12, f32[2,96]{1,0:T(2,128)} %bitcast.13), custom_call_target="tpu_custom_call" | custom-call | flops 1610612736 | bytes 8388608 | tf_op jit(solution)/shard_map/pallas_call | solution.py:388
  35.6 0.7 %shard_map.85 = (f32[4,96]{1,0:T(4,128)}, f32[32,96]{1,0:T(8,128)}, f32[2,96]{1,0:T(2,128)}, f32[2,96]{1,0:T(2,128)}) custom-call(f32[4,96]{1,0:T(4,128)S(1)} %get-tuple-element.12.refs_0_, f32[32,96]{1,0:T(8,128)S(1)} %get-tuple-element.13.refs_1_, f32[2,96]{1,0:T(2,128)S(1)} %get-tuple-element.14.refs_2_, f32[2,96]{1,0:T(2,128)S(1)} %get-tuple-element.15.refs_3_), custom_call_target="tpu_custom_call" | custom-call | tf_op jit(solution)/shard_map/pallas_call | solution.py:449

commit v13 on v12

--- a/solution.py
+++ b/solution.py
@@ -150,12 +150,12 @@
 
     pl.semaphore_wait(barrier, NY - 1 + NX - 1)
 
+    for to in core_peers:
+        send(colg.at[c, lz], colg.at[c, lz], S_COL, (a, to))
     for to in gy_peers:
         send(mine4, rowg.at[g], S_ROW, (a, to))
     for to in gx_peers:
         send(mine2, bandg.at[a], S_BAND, (to, g))
-    for to in core_peers:
-        send(colg.at[c, lz], colg.at[c, lz], S_COL, (a, to))
 
     @pl.loop(0, LOADS)
     def _(k):

time: 36.4 us -> 40.1 us (1.10)
  Pallas kernels: 35.6 us -> 39.3 us
    pallas_call x1, Pallas kernels: 35 us -> 38.7 us  [shards(): pl.pallas_call(kernel, out_shape=shapes, in_specs=[pl.BlockSpec(memory_sp...]
where the time goes in v13:
time: 40.1 us; the launch traced here: 40 us
  Pallas kernels  39.3 us (98%)
  between operations  0.64 us (2%)
    pallas_call x1, Pallas kernels, shards(): pl.pallas_call(kernel, out_shape=shapes, in_specs=[pl.BlockSpec(memory_sp...  38.7 us

profile of v13, /device:TPU:1, one launch (start us, length us, event | category | flops | bytes accessed | tf_op | source)
XLA Modules:
  0.0 40.0 jit_solution(6479194351503056978)
XLA Ops:
  0.6 38.7 %shard_map.84 = (f32[4,96]{1,0:T(4,128)S(1)}, f32[32,96]{1,0:T(8,128)S(1)}, f32[2,96]{1,0:T(2,128)S(1)}, f32[2,96]{1,0:T(2,128)S(1)}) custom-call(bf16[32,128,1024]{2,1,0:T(8,128)(2,1)} %bitcast.9, f32[4,96]{1,0:T(4,128)} %bitcast.11, f32[32,96]{1,0:T(8,128)} %bitcast.10, f32[2,96]{1,0:T(2,128)} %bitcast.12, f32[2,96]{1,0:T(2,128)} %bitcast.13), custom_call_target="tpu_custom_call" | custom-call | flops 1610612736 | bytes 8388608 | tf_op jit(solution)/shard_map/pallas_call | solution.py:388
  39.3 0.7 %shard_map.85 = (f32[4,96]{1,0:T(4,128)}, f32[32,96]{1,0:T(8,128)}, f32[2,96]{1,0:T(2,128)}, f32[2,96]{1,0:T(2,128)}) custom-call(f32[4,96]{1,0:T(4,128)S(1)} %get-tuple-element.12.refs_0_, f32[32,96]{1,0:T(8,128)S(1)} %get-tuple-element.13.refs_1_, f32[2,96]{1,0:T(2,128)S(1)} %get-tuple-element.14.refs_2_, f32[2,96]{1,0:T(2,128)S(1)} %get-tuple-element.15.refs_3_), custom_call_target="tpu_custom_call" | custom-call | tf_op jit(solution)/shard_map/pallas_call | solution.py:449

commit v14 on v13

--- a/solution.py
+++ b/solution.py
@@ -150,8 +150,6 @@
 
     pl.semaphore_wait(barrier, NY - 1 + NX - 1)
 
-    for to in core_peers:
-        send(colg.at[c, lz], colg.at[c, lz], S_COL, (a, to))
     for to in gy_peers:
         send(mine4, rowg.at[g], S_ROW, (a, to))
     for to in gx_peers:
@@ -165,6 +163,11 @@
         for i in range(per):
             at = pl.multiple_of((k * per + i) * ROWS, ROWS)
             turned[:, pl.ds(at, ROWS)] = data[k * per + i].T
+
+        @pl.when(k == 0)
+        def _():
+            for to in core_peers:
+                send(colg.at[c, lz], colg.at[c, lz], S_COL, (a, to))
 
     for to in gy_peers:
         send(mine2, bandx.at[g], S_BANDX, (a, to))

time: 40.1 us -> 35.7 us (0.89)
  Pallas kernels: 39.3 us -> 35 us
    pallas_call x1, Pallas kernels: 38.7 us -> 34.3 us  [shards(): pl.pallas_call(kernel, out_shape=shapes, in_specs=[pl.BlockSpec(memory_sp...]
where the time goes in v14:
time: 35.7 us; the launch traced here: 35.6 us
  Pallas kernels  35 us (98%)
  between operations  0.64 us (2%)
    pallas_call x1, Pallas kernels, shards(): pl.pallas_call(kernel, out_shape=shapes, in_specs=[pl.BlockSpec(memory_sp...  34.3 us

profile of v14, /device:TPU:1, one launch (start us, length us, event | category | flops | bytes accessed | tf_op | source)
XLA Modules:
  0.0 35.6 jit_solution(6239630267147767509)
XLA Ops:
  0.6 34.3 %shard_map.84 = (f32[4,96]{1,0:T(4,128)S(1)}, f32[32,96]{1,0:T(8,128)S(1)}, f32[2,96]{1,0:T(2,128)S(1)}, f32[2,96]{1,0:T(2,128)S(1)}) custom-call(bf16[32,128,1024]{2,1,0:T(8,128)(2,1)} %bitcast.9, f32[4,96]{1,0:T(4,128)} %bitcast.11, f32[32,96]{1,0:T(8,128)} %bitcast.10, f32[2,96]{1,0:T(2,128)} %bitcast.12, f32[2,96]{1,0:T(2,128)} %bitcast.13), custom_call_target="tpu_custom_call" | custom-call | flops 1610612736 | bytes 8388608 | tf_op jit(solution)/shard_map/pallas_call | solution.py:391
  35.0 0.7 %shard_map.85 = (f32[4,96]{1,0:T(4,128)}, f32[32,96]{1,0:T(8,128)}, f32[2,96]{1,0:T(2,128)}, f32[2,96]{1,0:T(2,128)}) custom-call(f32[4,96]{1,0:T(4,128)S(1)} %get-tuple-element.12.refs_0_, f32[32,96]{1,0:T(8,128)S(1)} %get-tuple-element.13.refs_1_, f32[2,96]{1,0:T(2,128)S(1)} %get-tuple-element.14.refs_2_, f32[2,96]{1,0:T(2,128)S(1)} %get-tuple-element.15.refs_3_), custom_call_target="tpu_custom_call" | custom-call | tf_op jit(solution)/shard_map/pallas_call | solution.py:452
